TPU v7x, 128 devices: a whole 4x4x4 slice. The times are simulated.
128 devices in a mesh: gx: 8 (over y, core), yz: 16 (over x, z).
Axes of the slice: x: 4, y: 4, z: 4, core: 2. Of those that a mesh axis runs over, the one named last changes fastest.
Arguments:
- composition: float32 [16384, 20, 128], P(('gx', 'yz')), may hold values from -6 to 6
- particle_mass: float32 [16384, 128], P(('gx', 'yz')), may hold values from 0.5 to 2
- mixing_rate: float32 [16384, 128], P(('gx', 'yz')), may hold values from 0.2 to 3
- cell_index: int32 [16384, 128], P(('gx', 'yz')), may hold values from 0 to 16383, as said below
- section_counts: int32 [16384], P(('gx', 'yz')), may hold values from 1 to 6, as said below
- block_shuffle: int32 [128, 128], P(('gx', 'yz')), may hold values from 0 to 127, as said below
- batch_inverse: float32 [128, 20, 20], P(('gx', 'yz')), may hold values from -1.25 to 1.25
- rate_exponents: float32 [84, 20], replicated, may hold values from -1.25 to 1.25
- stoichiometry: float32 [20, 84], replicated, may hold values from -0.625 to 0.625
Outputs:
- reacted: float32 [16384, 20, 128], P(('gx', 'yz'))
Inputs may be any that keep to these rules, and one draw needn't show every extreme that they name: `cell_index`: A particle of the device at index i of gx and j of yz (d = i * 16 + j) lies in slab i - 1, i or i + 1, slab s holding cells s * 128 * 16 to (s + 1) * 128 * 16 - 1; that device's first 128 particles lie one each in cells d * 128 to d * 128 + 127. `section_counts`: some block has exactly 6 sections. `block_shuffle`: each row is a permutation of 0 to 127.
All inputs are finite; a program needn't handle non-finite values.
Results may differ from a plain program's by a relative error of at most 0.0011.
Values sent between devices are 32-bit elements; how exact they have to be, the bound alone decides.
A program may use at most 128 MiB of HBM per device.

v0:
```python
import jax
import jax.numpy as jnp
from jax import lax
from jax.sharding import PartitionSpec as P

CELL_DEV = 128


step_size = 0.25


def extended_2(cells, sides, width):
    for axis, dim in sides:
        count = lax.axis_size(axis)
        ends = count - 1
        head = lax.slice_in_dim(cells, 0, width, axis=dim)
        tail = lax.slice_in_dim(cells, cells.shape[dim] - width, cells.shape[dim], axis=dim)
        cells = jnp.concatenate(
            [
                lax.ppermute(tail, axis, [(i, (i + 1) % count) for i in range(ends)]),
                cells,
                lax.ppermute(head, axis, [((i + 1) % count, i) for i in range(ends)]),
            ],
            axis=dim,
        )
    return cells


def section_update(current, matrices, rate_exponents, stoichiometry):
    progress = jnp.tanh(
        jnp.einsum("rj,bjk->brk", rate_exponents, current, precision=lax.Precision.HIGHEST)
    )
    forcing = jnp.einsum("ir,brk->bik", stoichiometry, progress, precision=lax.Precision.HIGHEST)
    return jnp.einsum("bij,bjk->bik", matrices, forcing, precision=lax.Precision.HIGHEST)


def advance_blocks(current, counts, matrices, rate_exponents, stoichiometry):
    ordering = jnp.argsort(-counts, stable=True)
    restore = jnp.argsort(ordering, stable=True)
    current = current[ordering]
    counts = counts[ordering]
    matrices = matrices[ordering]
    batch_width = min(current.shape[0], 64)

    def one_section(section_index, current):
        active = jnp.sum((counts > section_index).astype(jnp.int32))
        batches = (active + batch_width - 1) // batch_width

        def one_batch(number, current):
            offset = number * batch_width
            chosen = lax.dynamic_slice_in_dim(current, offset, batch_width, 0)
            chosen_matrices = lax.dynamic_slice_in_dim(matrices, offset, batch_width, 0)
            chosen_counts = lax.dynamic_slice_in_dim(counts, offset, batch_width, 0)
            updated = chosen + step_size * section_update(
                chosen, chosen_matrices, rate_exponents, stoichiometry
            )
            chosen = jnp.where((chosen_counts > section_index)[:, None, None], updated, chosen)
            return lax.dynamic_update_slice_in_dim(current, chosen, offset, 0)

        return lax.fori_loop(0, batches, one_batch, current)

    current = lax.fori_loop(0, jnp.max(counts), one_section, current)
    return current[restore]


def split_three(values):
    upper = values.astype(jnp.bfloat16)
    rest = values - upper.astype(jnp.float32)
    middle = rest.astype(jnp.bfloat16)
    lower = (rest - middle.astype(jnp.float32)).astype(jnp.bfloat16)
    return jnp.stack([upper, middle, lower], axis=0)


def local(
    composition,
    particle_mass,
    mixing_rate,
    cell_index,
    section_counts,
    block_shuffle,
    batch_inverse,
    rate_exponents,
    stoichiometry,
):
    block_total, species, lane_count = composition.shape
    columns = lax.axis_size("yz")
    slab_cells = CELL_DEV * columns
    first_cell = (lax.axis_index("gx") - 1) * slab_cells
    local_cell = cell_index - first_cell
    moments = species + 1
    low_width = min(256, slab_cells)
    high_count = 3 * slab_cells // low_width
    particles = block_total * lane_count
    tile = min(1024, particles)
    turns = particles // tile
    tile_blocks = tile // lane_count
    high_part = (local_cell // low_width).reshape(turns, tile)
    low_part = (local_cell % low_width).reshape(turns, tile)
    high_iota = jnp.arange(high_count, dtype=jnp.int32)
    low_iota = jnp.arange(low_width, dtype=jnp.int32)
    weighted = composition * particle_mass[:, None, :]
    values = jnp.concatenate([particle_mass[:, None, :], weighted], axis=1)
    values = (
        values.reshape(turns, tile_blocks, moments, lane_count)
        .transpose(0, 2, 1, 3)
        .reshape(turns, moments, tile)
    )

    def add_tile(number, total):
        pieces = split_three(values[number]).reshape(3 * moments, tile)
        high_table = (high_part[number][None, :] == high_iota[:, None]).astype(jnp.bfloat16)
        low_table = (low_part[number][:, None] == low_iota[None, :]).astype(jnp.bfloat16)
        spread = (pieces[:, None, :] * high_table[None, :, :]).reshape(
            3 * moments * high_count, tile
        )
        return total + jnp.dot(spread, low_table, preferred_element_type=jnp.float32)

    summed = lax.fori_loop(
        0, turns, add_tile, jnp.zeros((3 * moments * high_count, low_width), jnp.float32)
    )
    summed = summed.reshape(3, moments, 3 * slab_cells)
    partial_value = (
        (summed[0] + summed[1] + summed[2]).reshape(moments, 3, slab_cells).transpose(1, 0, 2)
    )
    reduced = lax.psum_scatter(partial_value, "yz", scatter_dimension=2, tiled=True)
    extended = extended_2(reduced, (("gx", 0),), 1)
    totals = extended[2] + extended[0] + extended[4]
    cell_means = totals[1:] / totals[0][None, :]
    gathered = lax.all_gather(cell_means[None], "yz", axis=2, tiled=True)
    nearby = extended_2(gathered, (("gx", 0),), 1)
    means_flat = jnp.moveaxis(nearby, 0, 1).reshape(species, 3 * slab_cells)
    mean_parts = split_three(means_flat).reshape(3, species * high_count, low_width)

    def look_tile(inputs):
        high_row, low_row = inputs
        low_table = (low_iota[:, None] == low_row[None, :]).astype(jnp.bfloat16)
        picked = jnp.dot(mean_parts[0], low_table, preferred_element_type=jnp.float32)
        picked = picked + jnp.dot(mean_parts[1], low_table, preferred_element_type=jnp.float32)
        picked = picked + jnp.dot(mean_parts[2], low_table, preferred_element_type=jnp.float32)
        high_table = (high_row[None, :] == high_iota[:, None]).astype(jnp.float32)
        return jnp.sum(picked.reshape(species, high_count, tile) * high_table[None], axis=1)

    looked = lax.map(look_tile, (high_part, low_part))
    looked = (
        looked.reshape(turns, species, tile_blocks, lane_count)
        .transpose(0, 2, 1, 3)
        .reshape(block_total, species, lane_count)
    )
    mixed_state = looked + (composition - looked) * jnp.exp(-mixing_rate)[:, None, :]
    ordering = block_shuffle[0]
    outgoing = mixed_state[ordering]
    outgoing_counts = section_counts[ordering].astype(jnp.float32)
    arrived, arrived_counts = (
        lax.all_to_all(outgoing, ("gx", "yz"), split_axis=0, concat_axis=0, tiled=True),
        lax.all_to_all(outgoing_counts, ("gx", "yz"), split_axis=0, concat_axis=0, tiled=True),
    )
    matrices = jnp.broadcast_to(batch_inverse[0], (block_total, species, species))
    reacted = advance_blocks(
        arrived, arrived_counts.astype(jnp.int32), matrices, rate_exponents, stoichiometry
    )
    returned = lax.all_to_all(reacted, ("gx", "yz"), split_axis=0, concat_axis=0, tiled=True)
    return returned[jnp.argsort(ordering, stable=True)]


def solution(mesh):
    in_specs = (
        P(("gx", "yz"), None, None),
        P(("gx", "yz"), None),
        P(("gx", "yz"), None),
        P(("gx", "yz"), None),
        P(("gx", "yz")),
        P(("gx", "yz"), None),
        P(("gx", "yz"), None, None),
        P(),
        P(),
    )
    out_specs = P(("gx", "yz"), None, None)
    return jax.shard_map(local, mesh=mesh, in_specs=in_specs, out_specs=out_specs, check_vma=False)
```

profile of v0, /device:TPU:1, one launch (start us, length us, event | category | flops | bytes accessed | tf_op | source)
XLA Modules:
  0.0 426.2 jit_solution(5385885713294950449)
XLA Ops:
  10.4 83.8 %while.68 = (s32[]{:T(128)}, f32[1512,256]{1,0:T(8,128)}, f32[16,21,1024]{2,0,1:T(8,128)}, s32[16,1024]{1,0:T(8,128)S(1)}, s32[16,1024]{1,0:T(8,128)S(1)}, /*index=5*/s32[]{:T(128)}, s32[]{:T(128)}) while((s32[]{:T(128)}, f32[1512,256]{1,0:T(8,128)}, f32[16,21,1024]{2,0,1:T(8,128)}, s32[16,1024]{1,0:T(8,128)S(1)}, ...), condition=%wide.region_1.2_spmd.clone, body=%wide.region_0.1_spmd.clone.sunk | while | flops 795636736 | bytes 10530911 | solution.py:118
  12.0 2.4 convolution_add_fusion.2
  15.9 3.8 convolution_add_fusion.2
  21.2 3.8 convolution_add_fusion.2
  26.6 3.8 convolution_add_fusion.2
  31.9 3.8 convolution_add_fusion.2
  37.2 3.8 convolution_add_fusion.2
  42.5 3.8 convolution_add_fusion.2
  47.9 3.8 convolution_add_fusion.2
  53.2 3.8 convolution_add_fusion.2
  58.5 3.8 convolution_add_fusion.2
  63.8 3.8 convolution_add_fusion.2
  69.2 3.8 convolution_add_fusion.2
  74.5 3.8 convolution_add_fusion.2
  79.8 3.8 convolution_add_fusion.2
  85.1 3.8 convolution_add_fusion.2
  90.5 3.8 convolution_add_fusion.2
  96.0 13.5 %copy.60 = f32[3,21,2048]{0,1,2:T(8,128)} copy(f32[3,21,2048]{2,0,1:T(4,128)S(1)} %bitcast.104) | data formatting | bytes 1032192
  109.4 15.1 %reshape.286 = f32[2048,63]{1,0:T(8,128)} reshape(f32[2048,21,3]{2,1,0:T(8,128)} %bitcast.101) | data formatting | bytes 1032192
  125.9 73.6 %reduce-scatter.4.cloned.1.call-done = f32[128,63]{1,0:T(8,128)} async-done(((f32[2048,63]{1,0:T(8,128)}), f32[128,63]{1,0:T(8,128)}) %reduce-scatter.4.cloned.1.call-update) | async-done | bytes 32272
  200.7 2.6 fusion.42
  203.3 1.9 copy.66
  205.2 5.3 %collective-permute-start = (f32[1,21,128]{2,0,1:T(1,128)S(1)}, f32[1,21,128]{2,0,1:T(1,128)S(1)}, u32[]{:S(2)}, u32[]{:S(2)}) collective-permute-start(f32[1,21,128]{2,0,1:T(1,128)S(1)} %copy.66), channel_id=1, source_target_pairs={{0,16},{16,32},{32,48},{48,64},{64,80},{80,96},{96,112},{1,17},{17... | collective-permute-start | bytes 32264 | tf_op jit(solution)/shard_map/ppermute | solution.py:20
  211.0 1.9 collective-permute-start.1
  213.6 7.5 %all-to-all-start.1 = ((f32[128,1,1]{2,1,0:T(1,128)}), f32[128,1,1]{2,1,0:T(1,128)S(1)}, u32[]{:S(2)}, u32[]{:S(2)}) async-start(f32[128,1,1]{2,1,0:T(1,128)} %copy.56), calls=%async_computation.1 | async-start | bytes 131072 | tf_op jit(solution)/shard_map/all_to_all | solution.py:155
  221.7 19.6 %all-gather = f32[20,2048]{1,0:T(8,128)S(1)} all-gather(f32[20,128]{1,0:T(8,128)S(1)} %bitcast_divide_fusion), channel_id=2, replica_groups=mesh['gx'=8,'yz'=16] {'yz'}, dimensions={1}, use_global_device_ids=true | all-gather | bytes 174080 | tf_op jit(solution)/shard_map/all_gather | solution.py:129
  241.3 8.7 %collective-permute-start.2 = (f32[1,20,2048]{2,1,0:T(8,128)S(1)}, f32[1,20,2048]{2,1,0:T(8,128)S(1)}, u32[]{:S(2)}, u32[]{:S(2)}) collective-permute-start(f32[1,20,2048]{2,1,0:T(8,128)S(1)} %bitcast.108), channel_id=1, source_target_pairs={{0,16},{16,32},{32,48},{48,64},{64,80},{80,96},{96,112},{1,17},{17... | collective-permute-start | bytes 491528 | tf_op jit(solution)/shard_map/ppermute | solution.py:20
  250.0 2.1 collective-permute-start.3
  252.6 4.4 %collective-permute-done.3 = f32[1,20,2048]{2,1,0:T(8,128)S(1)} collective-permute-done((f32[1,20,2048]{2,1,0:T(8,128)S(1)}, f32[1,20,2048]{2,1,0:T(8,128)S(1)}, u32[]{:S(2)}, u32[]{:S(2)}) %collective-permute-start.3) | collective-permute-done | bytes 163872 | tf_op jit(solution)/shard_map/ppermute | solution.py:22
  257.9 30.5 %while.67 = (s32[]{:T(128)}, f32[16,20,1024]{2,1,0:T(8,128)S(1)}, s32[16,1024]{1,0:T(8,128)S(1)}, bf16[3,480,256]{2,1,0:T(8,128)(2,1)S(1)}, s32[16,1024]{1,0:T(8,128)S(1)}, /*index=5*/s32[]{:T(128)}) while((s32[]{:T(128)}, f32[16,20,1024]{2,1,0:T(8,128)S(1)}, s32[16,1024]{1,0:T(8,128)S(1)}, bf16[3,480,256]{2,1,0:T(8,128)(2,1)S(1)}, ...), condition=%wide.region_5.6_spmd.clone, body=%wide.region_3.5_spmd.clone.sunk | while | flops 757755904 | bytes 13041741 | solution.py:143
  290.7 1.9 gather_fusion
  292.7 6.7 %all-to-all-start = ((f32[128,20,128]{2,1,0:T(8,128)}), f32[128,20,128]{2,1,0:T(8,128)}, u32[]{:S(2)}, u32[]{:S(2)}) async-start(f32[128,20,128]{2,1,0:T(8,128)} %gather_fusion), calls=%async_computation | async-start | bytes 3145728 | tf_op jit(solution)/shard_map/all_to_all | solution.py:154
  299.4 2.4 convert_reduce_fusion
  301.8 2.5 sort.45
  306.4 2.5 sort.46
  309.6 13.6 %all-to-all-done = f32[128,20,128]{2,1,0:T(8,128)} async-done(((f32[128,20,128]{2,1,0:T(8,128)}), f32[128,20,128]{2,1,0:T(8,128)}, u32[]{:S(2)}, u32[]{:S(2)}) %all-to-all-start) | async-done | bytes 1310752 | tf_op jit(solution)/shard_map/all_to_all | solution.py:154
  323.1 2.1 gather_fusion.2
  325.2 61.0 %while.66 = (s32[]{:T(128)}, f32[128,20,128]{2,1,0:T(8,128)S(1)}, s32[]{:T(128)}, s32[128]{0:T(128)S(1)}, f32[128,20,20]{2,1,0:T(8,128)S(1)}, /*index=5*/f32[84,...) while((s32[]{:T(128)}, f32[128,20,128]{2,1,0:T(8,128)S(1)}, ...), condition=%wide.region_12.13_spmd, body=%wide.region_8.12_spmd.sunk | while | flops 370115008 | bytes 10114534 | solution.py:62
  327.4 12.1 %while.69 = (s32[]{:T(128)}, f32[128,20,128]{2,1,0:T(8,128)S(1)}, s32[]{:T(128)}, s32[128]{0:T(128)S(1)}, s32[]{:T(128)}, /*index=5*/f32[128,20,20]{2,1,0:T(8,12...) while((s32[]{:T(128)}, f32[128,20,128]{2,1,0:T(8,128)S(1)}, ...), condition=%wide.region_11.11_spmd, body=%wide.region_10.10_spmd.sunk | while | flops 370114624 | bytes 10113583 | solution.py:60
  327.4 2.4 fusion.81
  329.9 2.1 fusion.82
  333.5 2.4 fusion.81
  335.9 2.1 fusion.82
  341.5 12.1 %while.69 = (s32[]{:T(128)}, f32[128,20,128]{2,1,0:T(8,128)S(1)}, s32[]{:T(128)}, s32[128]{0:T(128)S(1)}, s32[]{:T(128)}, /*index=5*/f32[128,20,20]{2,1,0:T(8,12...) while((s32[]{:T(128)}, f32[128,20,128]{2,1,0:T(8,128)S(1)}, ...), condition=%wide.region_11.11_spmd, body=%wide.region_10.10_spmd.sunk | while | flops 370114624 | bytes 10113583 | solution.py:60
  341.5 2.4 fusion.81
  344.0 2.1 fusion.82
  347.5 2.4 fusion.81
  350.0 2.1 fusion.82
  355.5 6.0 %while.69 = (s32[]{:T(128)}, f32[128,20,128]{2,1,0:T(8,128)S(1)}, s32[]{:T(128)}, s32[128]{0:T(128)S(1)}, s32[]{:T(128)}, /*index=5*/f32[128,20,20]{2,1,0:T(8,12...) while((s32[]{:T(128)}, f32[128,20,128]{2,1,0:T(8,128)S(1)}, ...), condition=%wide.region_11.11_spmd, body=%wide.region_10.10_spmd.sunk | while | flops 370114624 | bytes 10113583 | solution.py:60
  355.6 2.4 fusion.81
  358.0 2.1 fusion.82
  363.6 6.0 %while.69 = (s32[]{:T(128)}, f32[128,20,128]{2,1,0:T(8,128)S(1)}, s32[]{:T(128)}, s32[128]{0:T(128)S(1)}, s32[]{:T(128)}, /*index=5*/f32[128,20,20]{2,1,0:T(8,12...) while((s32[]{:T(128)}, f32[128,20,128]{2,1,0:T(8,128)S(1)}, ...), condition=%wide.region_11.11_spmd, body=%wide.region_10.10_spmd.sunk | while | flops 370114624 | bytes 10113583 | solution.py:60
  363.6 2.4 fusion.81
  366.0 2.1 fusion.82
  371.6 6.0 %while.69 = (s32[]{:T(128)}, f32[128,20,128]{2,1,0:T(8,128)S(1)}, s32[]{:T(128)}, s32[128]{0:T(128)S(1)}, s32[]{:T(128)}, /*index=5*/f32[128,20,20]{2,1,0:T(8,12...) while((s32[]{:T(128)}, f32[128,20,128]{2,1,0:T(8,128)S(1)}, ...), condition=%wide.region_11.11_spmd, body=%wide.region_10.10_spmd.sunk | while | flops 370114624 | bytes 10113583 | solution.py:60
  371.6 2.4 fusion.81
  374.1 2.1 fusion.82
  379.6 6.0 %while.69 = (s32[]{:T(128)}, f32[128,20,128]{2,1,0:T(8,128)S(1)}, s32[]{:T(128)}, s32[128]{0:T(128)S(1)}, s32[]{:T(128)}, /*index=5*/f32[128,20,20]{2,1,0:T(8,12...) while((s32[]{:T(128)}, f32[128,20,128]{2,1,0:T(8,128)S(1)}, ...), condition=%wide.region_11.11_spmd, body=%wide.region_10.10_spmd.sunk | while | flops 370114624 | bytes 10113583 | solution.py:60
  379.7 2.4 fusion.81
  382.1 2.1 fusion.82
  386.2 1.9 gather_fusion.5
  388.2 4.8 %all-to-all-start.2 = ((f32[128,20,128]{2,1,0:T(8,128)}), f32[128,20,128]{2,1,0:T(8,128)S(1)}, u32[]{:S(2)}, u32[]{:S(2)}) async-start(f32[128,20,128]{2,1,0:T(8,128)} %gather_fusion.5), calls=%async_computation.2 | async-start | bytes 3145728 | tf_op jit(solution)/shard_map/all_to_all | solution.py:161
  393.0 2.5 sort.47
  395.6 21.6 %all-to-all-done.2 = f32[128,20,128]{2,1,0:T(8,128)S(1)} async-done(((f32[128,20,128]{2,1,0:T(8,128)}), f32[128,20,128]{2,1,0:T(8,128)S(1)}, u32[]{:S(2)}, u32[]{:S(2)}) %all-to-all-start.2) | async-done | bytes 1310752 | tf_op jit(solution)/shard_map/all_to_all | solution.py:161
  (336 shorter events, 87.9 us)
Async XLA Ops:
  6.5 118.1 %copy-start = (s32[128]{0:T(128)S(1)}, s32[128]{0:T(128)}, u32[]{:S(2)}) copy-start(s32[128]{0:T(128)} %param.21) | copy-start | bytes 1540
  6.5 192.9 %reduce-scatter.4.cloned.1.call-start = ((), (), s32[]{:S(2)}) async-start(), calls=%async_computation.4 | async-start | bytes 1114112
  6.5 2.4 copy-start.6
  109.4 15.2 %copy-start.9 = (s32[1,128]{1,0:T(1,128)S(1)}, s32[1,128]{1,0:T(1,128)}, u32[]{:S(2)}) copy-start(s32[1,128]{1,0:T(1,128)} %param.22) | copy-start | bytes 1540
  203.3 7.2 %copy-start.4 = (f32[1,21,128]{0,1,2:T(8,128)S(1)}, f32[1,21,128]{0,1,2:T(8,128)}, u32[]{:S(2)}) copy-start(f32[1,21,128]{0,1,2:T(8,128)} %get-tuple-element.524) | copy-start | bytes 32260
  205.2 16.4 %collective-permute-start = (f32[1,21,128]{2,0,1:T(1,128)S(1)}, f32[1,21,128]{2,0,1:T(1,128)S(1)}, u32[]{:S(2)}, u32[]{:S(2)}) collective-permute-start(f32[1,21,128]{2,0,1:T(1,128)S(1)} %copy.66), channel_id=1, source_target_pairs={{0,16},{16,32},{32,48},{48,64},{64,80},{80,96},{96,112},{1,17},{17... | collective-permute-start | bytes 32264 | tf_op jit(solution)/shard_map/ppermute | solution.py:20
  210.5 41.6 %copy-start.7 = (f32[128,128]{1,0:T(8,128)S(1)}, f32[128,128]{1,0:T(8,128)}, u32[]{:S(2)}) copy-start(f32[128,128]{1,0:T(8,128)} %param.19) | copy-start | bytes 196612
  211.0 10.7 %collective-permute-start.1 = (f32[1,21,128]{2,0,1:T(1,128)S(1)}, f32[1,21,128]{2,0,1:T(1,128)S(1)}, u32[]{:S(2)}, u32[]{:S(2)}) collective-permute-start(f32[1,21,128]{2,0,1:T(1,128)S(1)} %copy.67), channel_id=1, source_target_pairs={{16,0},{32,16},{48,32},{64,48},{80,64},{96,80},{112,96},{17,1},{33... | collective-permute-start | bytes 32264 | tf_op jit(solution)/shard_map/ppermute | solution.py:22
  213.6 79.0 %all-to-all-start.1 = ((f32[128,1,1]{2,1,0:T(1,128)}), f32[128,1,1]{2,1,0:T(1,128)S(1)}, u32[]{:S(2)}, u32[]{:S(2)}) async-start(f32[128,1,1]{2,1,0:T(1,128)} %copy.56), calls=%async_computation.1 | async-start | bytes 131072 | tf_op jit(solution)/shard_map/all_to_all | solution.py:155
  241.3 11.3 %collective-permute-start.2 = (f32[1,20,2048]{2,1,0:T(8,128)S(1)}, f32[1,20,2048]{2,1,0:T(8,128)S(1)}, u32[]{:S(2)}, u32[]{:S(2)}) collective-permute-start(f32[1,20,2048]{2,1,0:T(8,128)S(1)} %bitcast.108), channel_id=1, source_target_pairs={{0,16},{16,32},{32,48},{48,64},{64,80},{80,96},{96,112},{1,17},{17... | collective-permute-start | bytes 491528 | tf_op jit(solution)/shard_map/ppermute | solution.py:20
  250.0 7.0 %collective-permute-start.3 = (f32[1,20,2048]{2,1,0:T(8,128)S(1)}, f32[1,20,2048]{2,1,0:T(8,128)S(1)}, u32[]{:S(2)}, u32[]{:S(2)}) collective-permute-start(f32[1,20,2048]{2,1,0:T(8,128)S(1)} %bitcast.109), channel_id=1, source_target_pairs={{16,0},{32,16},{48,32},{64,48},{80,64},{96,80},{112,96},{17,1},{33... | collective-permute-start | bytes 491528 | tf_op jit(solution)/shard_map/ppermute | solution.py:22
  288.6 1.3 copy-start.5
  292.7 6.7 %copy-start.8 = (f32[1,20,20]{2,0,1:T(1,128)S(1)}, f32[1,20,20]{2,0,1:T(1,128)}, u32[]{:S(2)}) copy-start(f32[1,20,20]{2,0,1:T(1,128)} %param.23) | copy-start | bytes 4804
  292.7 30.4 %all-to-all-start = ((f32[128,20,128]{2,1,0:T(8,128)}), f32[128,20,128]{2,1,0:T(8,128)}, u32[]{:S(2)}, u32[]{:S(2)}) async-start(f32[128,20,128]{2,1,0:T(8,128)} %gather_fusion), calls=%async_computation | async-start | bytes 3145728 | tf_op jit(solution)/shard_map/all_to_all | solution.py:154
  309.5 15.7 %copy-start.2 = (f32[84,20]{0,1:T(8,128)S(1)}, f32[84,20]{0,1:T(8,128)}, u32[]{:S(2)}) copy-start(f32[84,20]{0,1:T(8,128)} %param.24) | copy-start | bytes 20164
  309.6 15.7 %copy-start.3 = (f32[20,84]{1,0:T(8,128)S(1)}, f32[20,84]{1,0:T(8,128)}, u32[]{:S(2)}) copy-start(f32[20,84]{1,0:T(8,128)} %param.25) | copy-start | bytes 20164
  388.2 29.0 %all-to-all-start.2 = ((f32[128,20,128]{2,1,0:T(8,128)}), f32[128,20,128]{2,1,0:T(8,128)S(1)}, u32[]{:S(2)}, u32[]{:S(2)}) async-start(f32[128,20,128]{2,1,0:T(8,128)} %gather_fusion.5), calls=%async_computation.2 | async-start | bytes 3145728 | tf_op jit(solution)/shard_map/all_to_all | solution.py:161
  417.2 2.1 copy-start.1
Sparse Core Ops, SparseCore 0:
  124.7 74.7 reduce-scatter.3
where the time goes:
time: 428 us; the launch traced here: 426 us
  matrix products  129 us (30%)
  waiting for transfers between devices  114 us (27%)
  local copies, waits for them, and re-layouts  71.4 us (17%)
  starting transfers between devices  37 us (9%)
  other arithmetic  30.6 us (7%)
  blocking collectives  19.6 us (5%)
  between operations  13.8 us (3%)
  loops' own time  10.8 us (3%)
    unnamed x2, waiting for transfers between devices  73.6 us
    dot_general x16, matrix products, add_tile(): jnp.dot(spread, low_table, preferred_element_type=jnp.float32)  58.8 us
    unnamed x27, local copies, waits for them, and re-layouts  33.8 us
    all_to_all x1, waiting for transfers between devices, local(): lax.all_to_all(reacted, ('gx', 'yz'), split_axis=0, concat_axis=0, tiled=...  21.6 us
    all_gather x1, blocking collectives, local(): gathered = lax.all_gather(cell_means[None], 'yz', axis=2, tiled=True)  19.6 us
    dot_general x8, matrix products, section_update(): jnp.einsum('rj,bjk->brk', rate_exponents, current, precision=lax.Precisio...  19.5 us
    dynamic_slice x32, local copies, waits for them, and re-layouts, add_tile(): pieces = split_three(values[number]).reshape(3 * moments, tile)  18.9 us
    dot_general x8, matrix products, section_update(): jnp.einsum('ir,brk->bik', stoichiometry, progress, precision=lax.Precisio...  16.7 us
  transfers between devices with their start and end apart: 8, of which 5 were waited for; matrix products, arithmetic and copies ran while one was open for 12% of the time, Pallas kernels for 0%

commit v1 on v0

v1 whole, which is shorter than its diff:
```python
import functools

import jax
import jax.numpy as jnp
from jax import lax
from jax.experimental import pallas as pl
from jax.experimental.pallas import tpu as pltpu
from jax.sharding import PartitionSpec as P

f32, bf16 = jnp.float32, jnp.bfloat16
MESH = pl.DeviceIdType.MESH
VMEM = pl.BlockSpec(memory_space=pltpu.VMEM)
SMEM = pl.BlockSpec(memory_space=pltpu.SMEM)

NS, NR, LANES = 20, 84, 128
CELL_DEV = 128
COLUMNS = 16
SLAB = CELL_DEV * COLUMNS
LOW = 256
HIGHS = 3 * SLAB // LOW
ROWS = 24
STEPS = 88
TILE = 8
GROUP = 8
STEP_SIZE = 0.25


def split(x):
    upper = x.astype(bf16)
    return upper, (x - upper.astype(f32)).astype(bf16)


def mm(a, b):
    return jnp.dot(a, b, preferred_element_type=f32)


def moments_kernel(
    comp_ref, mass_ref, cell_ref, counts_ref, shuffle_ref,
    part_ref, plan_ref, spread_ref, low_ref, acc_ref,
):
    blocks = comp_ref.shape[0]
    first = (lax.axis_index("gx") - 1) * SLAB
    iota = lax.broadcasted_iota(jnp.int32, (LOW, LANES), 0).astype(f32).astype(bf16)
    one, zero = jnp.ones((), bf16), jnp.zeros((), bf16)
    acc_ref[...] = jnp.zeros_like(acc_ref)

    def prepare(t, slot):
        base = pl.multiple_of(t * TILE, TILE)
        cells = cell_ref[pl.ds(base, TILE), :] - first
        high = (cells >> 8).astype(f32)
        low = (cells & (LOW - 1)).astype(f32)
        masses = mass_ref[pl.ds(base, TILE), :]
        for j in range(TILE):
            lanes = slice(j * LANES, (j + 1) * LANES)
            mass = masses[j : j + 1, :]
            value = jnp.concatenate(
                [comp_ref[base + j] * mass, mass, jnp.zeros((ROWS - NS - 1, LANES), f32)], 0
            )
            upper = value.astype(bf16).astype(f32)
            values = jnp.concatenate([upper, value - upper], 0).astype(bf16)
            high_row = jnp.broadcast_to(high[j : j + 1, :], (2 * ROWS, LANES)).astype(bf16)
            low_row = jnp.broadcast_to(low[j : j + 1, :], (LOW, LANES)).astype(bf16)
            for h in range(HIGHS):
                spread_ref[slot, h * 2 * ROWS : (h + 1) * 2 * ROWS, lanes] = jnp.where(
                    high_row == jnp.asarray(h, bf16), values, zero
                )
            low_ref[slot, :, lanes] = jnp.where(low_row == iota, one, zero)

    def multiply(slot):
        acc_ref[...] += lax.dot_general(
            spread_ref[slot], low_ref[slot], (((1,), (1,)), ((), ())), preferred_element_type=f32
        )

    def two_tiles(i, carry):
        prepare(2 * i, 0)
        multiply(0)
        prepare(2 * i + 1, 1)
        multiply(1)
        return carry

    lax.fori_loop(0, blocks // TILE // 2, two_tiles, 0)
    for h in range(HIGHS):
        total = acc_ref[h * 48 : h * 48 + 24, :] + acc_ref[h * 48 + 24 : h * 48 + 48, :]
        part_ref[2 * h] = total[:, :CELL_DEV]
        part_ref[2 * h + 1] = total[:, CELL_DEV:]

    row = lax.broadcasted_iota(jnp.int32, (blocks, blocks), 0)
    lane = lax.broadcasted_iota(jnp.int32, (blocks, blocks), 1)
    row_f, lane_f = row.astype(f32), lane.astype(f32)
    eye = row == lane
    counts = counts_ref[...].astype(f32)
    shuffle = shuffle_ref[...].astype(f32)
    block_of = jnp.sum(jnp.where(eye, shuffle, 0.0), axis=1, keepdims=True)
    count_of = jnp.sum(jnp.where(block_of == lane_f, counts, 0.0), axis=1, keepdims=True)
    count_row = jnp.sum(jnp.where(eye, count_of, 0.0), axis=0, keepdims=True)
    ahead = (count_row > count_of) | ((count_row == count_of) & (lane < row))
    rank = jnp.sum(jnp.where(ahead, 1.0, 0.0), axis=1, keepdims=True)
    here = rank == lane_f
    rows = [jnp.sum(jnp.where(here, v, 0.0), axis=0, keepdims=True) for v in (row_f, block_of, count_of)]
    plan_ref[...] = jnp.concatenate(rows + [jnp.zeros((5, blocks), f32)], 0).astype(jnp.int32)


def moments(composition, mass, cell, counts, shuffle):
    blocks = composition.shape[0]
    return pl.pallas_call(
        moments_kernel,
        out_shape=(
            jax.ShapeDtypeStruct((2 * HIGHS, ROWS, CELL_DEV), f32),
            jax.ShapeDtypeStruct((8, blocks), jnp.int32),
        ),
        in_specs=[VMEM] * 5,
        out_specs=(VMEM, VMEM),
        scratch_shapes=[
            pltpu.VMEM((2, HIGHS * 2 * ROWS, TILE * LANES), bf16),
            pltpu.VMEM((2, LOW, TILE * LANES), bf16),
            pltpu.VMEM((HIGHS * 2 * ROWS, LOW), f32),
        ],
        compiler_params=pltpu.CompilerParams(vmem_limit_bytes=50 << 20),
    )(composition, mass, cell, counts, shuffle)


def exchange_kernel(
    n_gx, part_ref, near_ref, halo_ref, own_ref, sums_ref, mine_ref,
    halo_send, halo_recv, sum_send, sum_recv, mean_send, mean_recv, slab_send, slab_recv,
):
    i, j = lax.axis_index("gx"), lax.axis_index("yz")
    left, right = lax.rem(i + n_gx - 1, n_gx), lax.rem(i + 1, n_gx)

    def column(p):
        return lax.rem(j + p, COLUMNS)

    def send(src, dst, send_sem, recv_sem, target):
        copy = pltpu.make_async_remote_copy(
            src_ref=src, dst_ref=dst, send_sem=send_sem, recv_sem=recv_sem,
            device_id=target, device_id_type=MESH,
        )
        copy.start()
        return copy

    barrier = pltpu.get_barrier_semaphore()
    for target in [(left, j), (right, j)] + [(i, column(p)) for p in range(1, COLUMNS)]:
        pl.semaphore_signal(barrier, inc=1, device_id=target, device_id_type=MESH)
    pl.semaphore_wait(barrier, COLUMNS + 1)

    def slab(s):
        return pl.ds(s * COLUMNS, COLUMNS)

    copies = [
        send(part_ref.at[slab(0)], halo_ref.at[1], halo_send.at[0], halo_recv.at[0], (left, j)),
        send(part_ref.at[slab(2)], halo_ref.at[0], halo_send.at[1], halo_recv.at[1], (right, j)),
    ]
    for copy in copies:
        copy.wait()
    own_ref[...] = part_ref[slab(1)] + halo_ref[0] + halo_ref[1]

    copies = [
        send(own_ref.at[column(p)], sums_ref.at[p], sum_send.at[p], sum_recv.at[p], (i, column(p)))
        for p in range(1, COLUMNS)
    ]
    total = own_ref[j]
    for p, copy in enumerate(copies, 1):
        copy.wait()
        total = total + sums_ref[p]
    means = total[:NS] / total[NS : NS + 1]
    mine_ref[...] = jnp.concatenate([means, jnp.zeros((ROWS - NS, CELL_DEV), f32)], 0)

    copies = [
        send(mine_ref, near_ref.at[COLUMNS + j], mean_send.at[p], mean_recv.at[p], (i, column(p)))
        for p in range(1, COLUMNS)
    ]
    near_ref[COLUMNS + j] = mine_ref[...]
    for copy in copies:
        copy.wait()

    copies = [
        send(near_ref.at[slab(1)], near_ref.at[slab(2)], slab_send.at[0], slab_recv.at[0], (left, j)),
        send(near_ref.at[slab(1)], near_ref.at[slab(0)], slab_send.at[1], slab_recv.at[1], (right, j)),
    ]
    for copy in copies:
        copy.wait()


def exchange(n_gx, part):
    dma = pltpu.SemaphoreType.DMA
    return pl.pallas_call(
        functools.partial(exchange_kernel, n_gx),
        out_shape=jax.ShapeDtypeStruct(part.shape, f32),
        in_specs=[VMEM],
        out_specs=VMEM,
        scratch_shapes=[
            pltpu.VMEM((2, COLUMNS, ROWS, CELL_DEV), f32),
            pltpu.VMEM((COLUMNS, ROWS, CELL_DEV), f32),
            pltpu.VMEM((COLUMNS, ROWS, CELL_DEV), f32),
            pltpu.VMEM((ROWS, CELL_DEV), f32),
            dma((2,)), dma((2,)), dma((COLUMNS,)), dma((COLUMNS,)),
            dma((COLUMNS,)), dma((COLUMNS,)), dma((2,)), dma((2,)),
        ],
        compiler_params=pltpu.CompilerParams(
            collective_id=0, has_side_effects=True, vmem_limit_bytes=20 << 20
        ),
    )(part)


def finish_kernel(
    plan_ref, comp_ref, rate_ref, cell_ref, near_ref, rates_ref, mats_ref,
    out_ref, state_ref, means_ref, low_ref, pick_ref, pair_ref,
):
    blocks = comp_ref.shape[0]
    first = (lax.axis_index("gx") - 1) * SLAB
    iota = lax.broadcasted_iota(jnp.int32, (LOW, LANES), 0).astype(f32).astype(bf16)
    one, zero = jnp.ones((), bf16), jnp.zeros((), bf16)
    for h in range(HIGHS):
        upper, lower = split(jnp.concatenate([near_ref[2 * h], near_ref[2 * h + 1]], 1))
        means_ref[h * ROWS : (h + 1) * ROWS, :LOW] = upper
        means_ref[h * ROWS : (h + 1) * ROWS, LOW:] = lower

    def prepare(t, slot):
        base = pl.multiple_of(t * TILE, TILE)
        low = ((cell_ref[pl.ds(base, TILE), :] - first) & (LOW - 1)).astype(f32)
        for j in range(TILE):
            lanes = slice(j * LANES, (j + 1) * LANES)
            low_row = jnp.broadcast_to(low[j : j + 1, :], (LOW, LANES)).astype(bf16)
            table = jnp.where(low_row == iota, one, zero)
            low_ref[slot, :LOW, lanes] = table
            low_ref[slot, LOW:, lanes] = table

    def multiply(slot):
        pick_ref[slot] = mm(means_ref[...], low_ref[slot])

    def mix(t, slot):
        base = pl.multiple_of(t * TILE, TILE)
        high = (cell_ref[pl.ds(base, TILE), :] - first) >> 8
        decay = jnp.exp(-rate_ref[pl.ds(base, TILE), :])
        for j in range(TILE):
            lanes = slice(j * LANES, (j + 1) * LANES)
            high_row = jnp.broadcast_to(high[j : j + 1, :], (ROWS, LANES))
            mean = jnp.zeros((ROWS, LANES), f32)
            for h in range(HIGHS):
                mean = jnp.where(high_row == h, pick_ref[slot, h * ROWS : (h + 1) * ROWS, lanes], mean)
            mean = mean[:NS]
            state_ref[base + j, :NS] = mean + (comp_ref[base + j] - mean) * decay[j : j + 1, :]
            state_ref[base + j, NS:] = jnp.zeros((ROWS - NS, LANES), f32)

    def two_tiles(i, carry):
        prepare(2 * i, 0)
        multiply(0)
        mix(2 * i, 0)
        prepare(2 * i + 1, 1)
        multiply(1)
        mix(2 * i + 1, 1)
        return carry

    lax.fori_loop(0, blocks // TILE // 2, two_tiles, 0)
    rates = rates_ref[...]

    def group(g, carry):
        at = [g * GROUP + b for b in range(GROUP)]
        block = [plan_ref[1, a] for a in at]
        need = [plan_ref[2, a] for a in at]
        for b in range(GROUP):
            upper, lower = split(mats_ref[plan_ref[0, at[b]]])
            pair_ref[b] = jnp.concatenate([upper.astype(f32), lower.astype(f32)], 0).astype(bf16)
        pairs = [pair_ref[b][:, :STEPS] for b in range(GROUP)]

        def section(s, states):
            after = []
            for b in range(0, GROUP, 2):
                x = jnp.concatenate(states[b : b + 2], 1)
                upper = x.astype(bf16).astype(f32)
                parts = jnp.concatenate([upper, x - upper, upper], 0).astype(bf16)
                t_upper, t_lower = split(jnp.tanh(mm(rates, parts)))
                y = mm(jnp.concatenate(pairs[b : b + 2], 0), t_upper)
                z = mm(jnp.concatenate([pairs[b][:ROWS], pairs[b + 1][:ROWS]], 0), t_lower)
                first_change = y[:24, :LANES] + y[24:48, :LANES] + z[:24, :LANES]
                second_change = y[48:72, LANES:] + y[72:, LANES:] + z[24:, LANES:]
                after.append(jnp.where(s < need[b], states[b] + first_change, states[b]))
                after.append(jnp.where(s < need[b + 1], states[b + 1] + second_change, states[b + 1]))
            return tuple(after)

        states = lax.fori_loop(0, need[0], section, tuple(state_ref[b] for b in block))
        for b in range(GROUP):
            out_ref[block[b]] = states[b][:NS]
        return carry

    lax.fori_loop(0, blocks // GROUP, group, 0)


def finish(plan, composition, rate, cell, near, rates, mats):
    return pl.pallas_call(
        finish_kernel,
        out_shape=jax.ShapeDtypeStruct(composition.shape, f32),
        in_specs=[SMEM] + [VMEM] * 6,
        out_specs=VMEM,
        scratch_shapes=[
            pltpu.VMEM((composition.shape[0], ROWS, LANES), f32),
            pltpu.VMEM((HIGHS * ROWS, 2 * LOW), bf16),
            pltpu.VMEM((2, 2 * LOW, TILE * LANES), bf16),
            pltpu.VMEM((2, HIGHS * ROWS, TILE * LANES), f32),
            pltpu.VMEM((GROUP, 2 * ROWS, LANES), bf16),
        ],
        compiler_params=pltpu.CompilerParams(vmem_limit_bytes=50 << 20),
    )(plan, composition, rate, cell, near, rates, mats)


def local(
    n_gx, composition, particle_mass, mixing_rate, cell_index, section_counts,
    block_shuffle, batch_inverse, rate_exponents, stoichiometry,
):
    mat = STEP_SIZE * jnp.dot(batch_inverse[0], stoichiometry, precision=lax.Precision.HIGHEST)
    mat = jnp.pad(mat, ((0, ROWS - NS), (0, LANES - NR)))
    mats = lax.all_gather(mat, ("gx", "yz"), axis=0)
    rates = jnp.pad(rate_exponents, ((0, STEPS - NR), (0, ROWS - NS)))
    upper = lax.reduce_precision(rates, 8, 7)
    rates = jnp.concatenate([upper, upper, rates - upper], 1).astype(bf16)
    part, plan = moments(composition, particle_mass, cell_index, section_counts[None], block_shuffle)
    near = exchange(n_gx, part)
    return finish(plan, composition, mixing_rate, cell_index, near, rates, mats)


def solution(mesh):
    both = ("gx", "yz")
    in_specs = (
        P(both, None, None), P(both, None), P(both, None), P(both, None), P(both),
        P(both, None), P(both, None, None), P(), P(),
    )
    return jax.shard_map(
        functools.partial(local, mesh.shape["gx"]),
        mesh=mesh, in_specs=in_specs, out_specs=P(both, None, None), check_vma=False,
    )
```

time: 428 us -> 151 us (0.35)
  matrix products: 129 us -> 0.84 us
  Pallas kernels: 0 us -> 106 us
  waiting for transfers between devices: 114 us -> 24.8 us
  local copies, waits for them, and re-layouts: 71.4 us -> 5.48 us
  starting transfers between devices: 37 us -> 0.04 us
  other arithmetic: 30.6 us -> 0.1 us
  blocking collectives: 19.6 us -> 0 us
  loops' own time: 10.8 us -> 0 us
    dot_general x88 -> x1, matrix products: 129 us -> 0.84 us  [local(): jnp.dot(batch_inverse[0], stoichiometry, precision=lax.Precision.HIGHEST)]
    pallas_call x0 -> x3, Pallas kernels: none -> 106 us  [the longest x1 64.1 us: finish(): pl.pallas_call(finish_kernel, out_shape=jax.ShapeDtypeStruct(composition....]
    unnamed x2 -> x1, waiting for transfers between devices: 73.6 us -> 0.02 us
    all_to_all x3 -> x0, waiting for transfers between devices: 35.2 us -> none  [the longest x1 21.6 us: local(): lax.all_to_all(reacted, ('gx', 'yz'), split_axis=0, concat_axis=0, tiled=...]
    unnamed x27 -> x14, local copies, waits for them, and re-layouts: 33.8 us -> 3.57 us
    all_gather x0 -> x1, waiting for transfers between devices: none -> 24.8 us  [local(): mats = lax.all_gather(mat, ('gx', 'yz'), axis=0)]
    all_gather x1 -> x0, blocking collectives: 19.6 us -> none  [local(): gathered = lax.all_gather(cell_means[None], 'yz', axis=2, tiled=True)]
    dynamic_slice x64 -> x0, local copies, waits for them, and re-layouts: 19.4 us -> none  [the longest x32 18.9 us: add_tile(): pieces = split_three(values[number]).reshape(3 * moments, tile)]
  transfers between devices with their start and end apart: 8 -> 1, of which waited for: 5 -> 1; matrix products, arithmetic and copies ran while one was open for 12% -> 2% of each run, Pallas kernels for 0% -> 28%
where the time goes in v1:
time: 151 us; the launch traced here: 150 us
  Pallas kernels  106 us (70%)
  waiting for transfers between devices  24.8 us (16%)
  between operations  13.5 us (9%)
  local copies, waits for them, and re-layouts  5.48 us (4%)
    pallas_call x1, Pallas kernels, finish(): pl.pallas_call(finish_kernel, out_shape=jax.ShapeDtypeStruct(composition....  64.1 us
    pallas_call x1, Pallas kernels, exchange(): pl.pallas_call(functools.partial(exchange_kernel, n_gx), out_shape=jax.Sh...  28.1 us
    all_gather x1, waiting for transfers between devices, local(): mats = lax.all_gather(mat, ('gx', 'yz'), axis=0)  24.8 us
    pallas_call x1, Pallas kernels, moments(): pl.pallas_call(moments_kernel, out_shape=(jax.ShapeDtypeStruct((2 * HIGHS...  13.3 us
    unnamed x14, local copies, waits for them, and re-layouts  3.57 us
  transfers between devices with their start and end apart: 1, of which 1 were waited for; matrix products, arithmetic and copies ran while one was open for 2% of the time, Pallas kernels for 28%

profile of v1, /device:TPU:1, one launch (start us, length us, event | category | flops | bytes accessed | tf_op | source)
XLA Modules:
  0.0 150.3 jit_solution(8159613291561625672)
XLA Ops:
  6.5 0.0 copy-start
  6.5 0.0 copy-start.1
  6.5 0.0 copy-start.5
  6.5 0.0 copy-start.4
  6.5 0.0 copy-start.3
  6.5 0.0 all-gather.3.cloned.1.call-start
  6.6 0.6 copy-done
  7.2 0.8 convolution_multiply_fusion
  8.1 0.6 pad.9
  8.7 0.0 all-gather.3.cloned.1.call-update
  8.7 0.8 copy.15
  9.5 2.1 %copy.14.comp_ref = f32[128,20,128]{2,1,0:T(8,128)S(1)} copy(f32[128,20,128]{2,0,1:T(8,128)} %param.9) | data formatting | bytes 2621440 | tf_op args[0]
  11.6 0.0 copy-start.2
  11.6 0.0 copy-done.1
  11.7 0.0 copy-done.5
  11.7 0.0 copy-done.4
  11.7 0.0 copy-done.3
  11.7 13.3 %shard_map.91 = (f32[48,24,128]{2,1,0:T(8,128)S(1)}, s32[8,128]{1,0:T(8,128)S(1)}) custom-call(f32[128,20,128]{2,1,0:T(8,128)S(1)} %copy.14.comp_ref, f32[128,128]{1,0:T(8,128)S(1)} %copy-done.3, s32[128,128]{1,0:T(8,128)S(1)} %copy-done.1, s32[1,128]{1,0:T(1,128)S(1)} %bitcast.6, s32[1,128]{1,0:T(1,128)S(1)} %copy-done.5), custom_call_target="tpu_custom_call" | custom-call | tf_op jit(solution)/shard_map/pallas_call | solution.py:105
  25.0 28.1 %shard_map.92.near_ref = f32[48,24,128]{2,1,0:T(8,128)S(1)} custom-call(f32[48,24,128]{2,1,0:T(8,128)S(1)} %get-tuple-element.8.part_ref), custom_call_target="tpu_custom_call" | custom-call | tf_op jit(solution)/shard_map/pallas_call | solution.py:185
  53.1 0.1 pad_maximum_fusion.rates_ref
  53.2 24.8 %all-gather.3.cloned.1.call-done = f32[3072,128]{1,0:T(8,128)} async-done(((f32[24,128]{1,0:T(8,128)}), f32[3072,128]{1,0:T(8,128)}) %all-gather.3.cloned.1.call-update) | async-done | bytes 1572880 | tf_op jit(solution)/shard_map/all_gather | solution.py:311
  78.0 0.0 copy-done.2
  78.0 64.1 %shard_map.93 = f32[128,20,128]{2,1,0:T(8,128)S(1)} custom-call(s32[8,128]{1,0:T(8,128)S(1)} %get-tuple-element.7.plan_ref, f32[128,20,128]{2,1,0:T(8,128)S(1)} %copy.14.comp_ref, f32[128,128]{1,0:T(8,128)S(1)} %copy-done.2, s32[128,128]{1,0:T(8,128)S(1)} %copy-done.1, f32[48,24,128]{2,1,0:T(8,128)S(1)} %shard_map.92.near_ref, ...), custom_call_target="tpu_custom_call" | custom-call | tf_op jit(solution)/shard_map/pallas_call | solution.py:289
  142.2 1.3 copy.17
  (1 shorter events, 0.0 us)
Async XLA Ops:
  6.5 0.7 copy-start
  6.5 5.1 %copy-start.1 = (s32[128,128]{1,0:T(8,128)S(1)}, s32[128,128]{1,0:T(8,128)}, u32[]{:S(2)}) copy-start(s32[128,128]{1,0:T(8,128)} %cell_ref.3) | copy-start | bytes 196612
  6.5 5.1 %copy-start.5 = (s32[1,128]{1,0:T(1,128)S(1)}, s32[1,128]{1,0:T(1,128)}, u32[]{:S(2)}) copy-start(s32[1,128]{1,0:T(1,128)} %shuffle_ref.1) | copy-start | bytes 1540
  6.5 5.1 %copy-start.4 = (s32[128]{0:T(128)S(1)}, s32[128]{0:T(128)}, u32[]{:S(2)}) copy-start(s32[128]{0:T(128)} %param.13) | copy-start | bytes 1540
  6.5 5.1 %copy-start.3 = (f32[128,128]{1,0:T(8,128)S(1)}, f32[128,128]{1,0:T(8,128)}, u32[]{:S(2)}) copy-start(f32[128,128]{1,0:T(8,128)} %mass_ref.1) | copy-start | bytes 196612
  6.5 71.5 %all-gather.3.cloned.1.call-start = ((), (), s32[]{:S(2)}) async-start(), calls=%async_computation | async-start | bytes 1585152 | tf_op jit(solution)/shard_map/all_gather | solution.py:311
  11.6 66.4 %copy-start.2 = (f32[128,128]{1,0:T(8,128)S(1)}, f32[128,128]{1,0:T(8,128)}, u32[]{:S(2)}) copy-start(f32[128,128]{1,0:T(8,128)} %rate_ref.1) | copy-start | bytes 196612
Sparse Core Ops, SparseCore 0:
  10.2 67.8 all-gather.2

commit v2 on v1

--- a/solution.py
+++ b/solution.py
@@ -21,8 +21,9 @@
 ROWS = 24
 STEPS = 88
 TILE = 8
-GROUP = 8
+GROUP = 32
 STEP_SIZE = 0.25
+PACK = 4
 
 
 def split(x):
@@ -86,7 +87,8 @@
 
     row = lax.broadcasted_iota(jnp.int32, (blocks, blocks), 0)
     lane = lax.broadcasted_iota(jnp.int32, (blocks, blocks), 1)
-    row_f, lane_f = row.astype(f32), lane.astype(f32)
+    lane_f = lane.astype(f32)
+    place = ((row % COLUMNS) * (blocks // COLUMNS) + row // COLUMNS).astype(f32)
     eye = row == lane
     counts = counts_ref[...].astype(f32)
     shuffle = shuffle_ref[...].astype(f32)
@@ -96,7 +98,7 @@
     ahead = (count_row > count_of) | ((count_row == count_of) & (lane < row))
     rank = jnp.sum(jnp.where(ahead, 1.0, 0.0), axis=1, keepdims=True)
     here = rank == lane_f
-    rows = [jnp.sum(jnp.where(here, v, 0.0), axis=0, keepdims=True) for v in (row_f, block_of, count_of)]
+    rows = [jnp.sum(jnp.where(here, v, 0.0), axis=0, keepdims=True) for v in (place, block_of, count_of)]
     plan_ref[...] = jnp.concatenate(rows + [jnp.zeros((5, blocks), f32)], 0).astype(jnp.int32)
 
 
@@ -120,14 +122,19 @@
 
 
 def exchange_kernel(
-    n_gx, part_ref, near_ref, halo_ref, own_ref, sums_ref, mine_ref,
+    n_gx, part_ref, packed_ref, stoich_ref, near_ref, mats_ref,
+    halo_ref, own_ref, sums_ref, mine_ref, batch_ref, wide_ref,
     halo_send, halo_recv, sum_send, sum_recv, mean_send, mean_recv, slab_send, slab_recv,
+    row_send, row_recv, batch_send, batch_recv,
 ):
     i, j = lax.axis_index("gx"), lax.axis_index("yz")
     left, right = lax.rem(i + n_gx - 1, n_gx), lax.rem(i + 1, n_gx)
 
     def column(p):
         return lax.rem(j + p, COLUMNS)
+
+    def gx_peer(p):
+        return lax.rem(i + p, n_gx)
 
     def send(src, dst, send_sem, recv_sem, target):
         copy = pltpu.make_async_remote_copy(
@@ -137,28 +144,47 @@
         copy.start()
         return copy
 
-    barrier = pltpu.get_barrier_semaphore()
-    for target in [(left, j), (right, j)] + [(i, column(p)) for p in range(1, COLUMNS)]:
-        pl.semaphore_signal(barrier, inc=1, device_id=target, device_id_type=MESH)
-    pl.semaphore_wait(barrier, COLUMNS + 1)
-
     def slab(s):
         return pl.ds(s * COLUMNS, COLUMNS)
 
-    copies = [
+    barrier = pltpu.get_barrier_semaphore()
+    peers = [(gx_peer(p), j) for p in range(1, n_gx)] + [(i, column(p)) for p in range(1, COLUMNS)]
+    for target in peers:
+        pl.semaphore_signal(barrier, inc=1, device_id=target, device_id_type=MESH)
+    batch_ref[j, i] = packed_ref[...]
+    pl.semaphore_wait(barrier, len(peers))
+
+    halos = [
         send(part_ref.at[slab(0)], halo_ref.at[1], halo_send.at[0], halo_recv.at[0], (left, j)),
         send(part_ref.at[slab(2)], halo_ref.at[0], halo_send.at[1], halo_recv.at[1], (right, j)),
     ]
-    for copy in copies:
+    rows = [
+        send(batch_ref.at[j, i], batch_ref.at[j, i], row_send.at[p], row_recv.at[p], (gx_peer(p), j))
+        for p in range(1, n_gx)
+    ]
+    for copy in halos:
         copy.wait()
     own_ref[...] = part_ref[slab(1)] + halo_ref[0] + halo_ref[1]
 
-    copies = [
+    partials = [
         send(own_ref.at[column(p)], sums_ref.at[p], sum_send.at[p], sum_recv.at[p], (i, column(p)))
         for p in range(1, COLUMNS)
     ]
+    for copy in rows:
+        copy.wait()
+    batches = [
+        send(batch_ref.at[j], batch_ref.at[j], batch_send.at[p], batch_recv.at[p], (i, column(p)))
+        for p in range(1, COLUMNS)
+    ]
+    wide_ref[...] = jnp.zeros_like(wide_ref)
+    upper, lower = (v.astype(f32) for v in split(STEP_SIZE * stoich_ref[...]))
+    for c in range(NS // PACK):
+        lanes = slice(c * LANES, c * LANES + NR)
+        for k, piece in enumerate((upper, lower, upper)):
+            wide_ref[k * LANES + c * ROWS : k * LANES + c * ROWS + NS, lanes] = piece
+
     total = own_ref[j]
-    for p, copy in enumerate(copies, 1):
+    for p, copy in enumerate(partials, 1):
         copy.wait()
         total = total + sums_ref[p]
     means = total[:NS] / total[NS : NS + 1]
@@ -172,38 +198,56 @@
     for copy in copies:
         copy.wait()
 
-    copies = [
+    slabs = [
         send(near_ref.at[slab(1)], near_ref.at[slab(2)], slab_send.at[0], slab_recv.at[0], (left, j)),
         send(near_ref.at[slab(1)], near_ref.at[slab(0)], slab_send.at[1], slab_recv.at[1], (right, j)),
     ]
-    for copy in copies:
-        copy.wait()
-
-
-def exchange(n_gx, part):
+
+    for copy in batches:
+        copy.wait()
+    wide = wide_ref[...].astype(bf16)
+    batch_total = n_gx * COLUMNS
+    for t in range(PACK):
+        upper, lower = split(batch_ref[:, :, t, :].reshape(batch_total, LANES))
+        product = mm(jnp.concatenate([upper, upper, lower], 1), wide)
+        for c in range(NS // PACK):
+            mats_ref[:, PACK * c + t, :] = product[:, c * LANES : (c + 1) * LANES]
+    for r in range(NS, ROWS):
+        mats_ref[:, r, :] = jnp.zeros((batch_total, LANES), f32)
+    for copy in slabs:
+        copy.wait()
+
+
+def exchange(n_gx, part, packed, stoichiometry):
     dma = pltpu.SemaphoreType.DMA
     return pl.pallas_call(
         functools.partial(exchange_kernel, n_gx),
-        out_shape=jax.ShapeDtypeStruct(part.shape, f32),
-        in_specs=[VMEM],
-        out_specs=VMEM,
+        out_shape=(
+            jax.ShapeDtypeStruct(part.shape, f32),
+            jax.ShapeDtypeStruct((n_gx * COLUMNS, ROWS, LANES), f32),
+        ),
+        in_specs=[VMEM] * 3,
+        out_specs=(VMEM, VMEM),
         scratch_shapes=[
             pltpu.VMEM((2, COLUMNS, ROWS, CELL_DEV), f32),
             pltpu.VMEM((COLUMNS, ROWS, CELL_DEV), f32),
             pltpu.VMEM((COLUMNS, ROWS, CELL_DEV), f32),
             pltpu.VMEM((ROWS, CELL_DEV), f32),
+            pltpu.VMEM((COLUMNS, n_gx, PACK, LANES), f32),
+            pltpu.VMEM((3 * LANES, NS // PACK * LANES), f32),
             dma((2,)), dma((2,)), dma((COLUMNS,)), dma((COLUMNS,)),
             dma((COLUMNS,)), dma((COLUMNS,)), dma((2,)), dma((2,)),
+            dma((n_gx,)), dma((n_gx,)), dma((COLUMNS,)), dma((COLUMNS,)),
         ],
         compiler_params=pltpu.CompilerParams(
             collective_id=0, has_side_effects=True, vmem_limit_bytes=20 << 20
         ),
-    )(part)
+    )(part, packed, stoichiometry)
 
 
 def finish_kernel(
     plan_ref, comp_ref, rate_ref, cell_ref, near_ref, rates_ref, mats_ref,
-    out_ref, state_ref, means_ref, low_ref, pick_ref, pair_ref,
+    out_ref, state_ref, means_ref, low_ref, pick_ref, pair_ref, turn_ref,
 ):
     blocks = comp_ref.shape[0]
     first = (lax.axis_index("gx") - 1) * SLAB
@@ -251,28 +295,42 @@
         return carry
 
     lax.fori_loop(0, blocks // TILE // 2, two_tiles, 0)
-    rates = rates_ref[...]
+    turn_ref[...] = jnp.zeros_like(turn_ref)
+    upper, lower = (v.astype(f32) for v in split(rates_ref[...]))
+    for k, piece in enumerate((upper, upper, lower)):
+        turn_ref[k * ROWS : k * ROWS + NS, :NR] = piece
+    rates = turn_ref[...].T[:STEPS, : 3 * ROWS].astype(bf16)
+    lane = lax.broadcasted_iota(jnp.int32, (ROWS, LANES), 1)
 
     def group(g, carry):
         at = [g * GROUP + b for b in range(GROUP)]
         block = [plan_ref[1, a] for a in at]
         need = [plan_ref[2, a] for a in at]
         for b in range(GROUP):
-            upper, lower = split(mats_ref[plan_ref[0, at[b]]])
-            pair_ref[b] = jnp.concatenate([upper.astype(f32), lower.astype(f32)], 0).astype(bf16)
-        pairs = [pair_ref[b][:, :STEPS] for b in range(GROUP)]
+            upper, lower = (v.astype(f32) for v in split(mats_ref[plan_ref[0, at[b]]]))
+            turned = pltpu.roll(upper, STEPS, 1)
+            head = jnp.where(lane < STEPS, upper, turned)
+            tail = jnp.where(lane < 2 * STEPS - LANES, turned, 0.0)
+            pair_ref[b, :, :LANES] = jnp.concatenate([head, lower], 0).astype(bf16)
+            pair_ref[b, :, LANES:] = jnp.concatenate([tail, jnp.zeros((ROWS, LANES), f32)], 0).astype(bf16)
 
         def section(s, states):
+            x = jnp.concatenate(states, 1)
+            upper = x.astype(bf16).astype(f32)
+            progress = jnp.tanh(mm(rates, jnp.concatenate([upper, x - upper, upper], 0).astype(bf16)))
+            upper = progress.astype(bf16).astype(f32)
+            progress = jnp.concatenate([upper, progress - upper], 0).astype(bf16)
+            products = [
+                mm(
+                    pair_ref[b : b + 2].reshape(4 * ROWS, 2 * LANES)[:, : 2 * STEPS],
+                    progress[:, b * LANES : (b + 2) * LANES],
+                )
+                for b in range(0, GROUP, 2)
+            ]
             after = []
-            for b in range(0, GROUP, 2):
-                x = jnp.concatenate(states[b : b + 2], 1)
-                upper = x.astype(bf16).astype(f32)
-                parts = jnp.concatenate([upper, x - upper, upper], 0).astype(bf16)
-                t_upper, t_lower = split(jnp.tanh(mm(rates, parts)))
-                y = mm(jnp.concatenate(pairs[b : b + 2], 0), t_upper)
-                z = mm(jnp.concatenate([pairs[b][:ROWS], pairs[b + 1][:ROWS]], 0), t_lower)
-                first_change = y[:24, :LANES] + y[24:48, :LANES] + z[:24, :LANES]
-                second_change = y[48:72, LANES:] + y[72:, LANES:] + z[24:, LANES:]
+            for b, y in zip(range(0, GROUP, 2), products):
+                first_change = y[:24, :LANES] + y[24:48, :LANES]
+                second_change = y[48:72, LANES:] + y[72:, LANES:]
                 after.append(jnp.where(s < need[b], states[b] + first_change, states[b]))
                 after.append(jnp.where(s < need[b + 1], states[b + 1] + second_change, states[b + 1]))
             return tuple(after)
@@ -296,7 +354,8 @@
             pltpu.VMEM((HIGHS * ROWS, 2 * LOW), bf16),
             pltpu.VMEM((2, 2 * LOW, TILE * LANES), bf16),
             pltpu.VMEM((2, HIGHS * ROWS, TILE * LANES), f32),
-            pltpu.VMEM((GROUP, 2 * ROWS, LANES), bf16),
+            pltpu.VMEM((GROUP, 2 * ROWS, 2 * LANES), bf16),
+            pltpu.VMEM((LANES, LANES), f32),
         ],
         compiler_params=pltpu.CompilerParams(vmem_limit_bytes=50 << 20),
     )(plan, composition, rate, cell, near, rates, mats)
@@ -306,15 +365,12 @@
     n_gx, composition, particle_mass, mixing_rate, cell_index, section_counts,
     block_shuffle, batch_inverse, rate_exponents, stoichiometry,
 ):
-    mat = STEP_SIZE * jnp.dot(batch_inverse[0], stoichiometry, precision=lax.Precision.HIGHEST)
-    mat = jnp.pad(mat, ((0, ROWS - NS), (0, LANES - NR)))
-    mats = lax.all_gather(mat, ("gx", "yz"), axis=0)
-    rates = jnp.pad(rate_exponents, ((0, STEPS - NR), (0, ROWS - NS)))
-    upper = lax.reduce_precision(rates, 8, 7)
-    rates = jnp.concatenate([upper, upper, rates - upper], 1).astype(bf16)
     part, plan = moments(composition, particle_mass, cell_index, section_counts[None], block_shuffle)
-    near = exchange(n_gx, part)
-    return finish(plan, composition, mixing_rate, cell_index, near, rates, mats)
+    packed = jnp.pad(batch_inverse[0], ((0, 0), (0, ROWS - NS)))
+    packed = packed.reshape(NS // PACK, PACK, ROWS).transpose(1, 0, 2).reshape(PACK, NS // PACK * ROWS)
+    packed = jnp.pad(packed, ((0, 0), (0, LANES - NS // PACK * ROWS)))
+    near, mats = exchange(n_gx, part, packed, stoichiometry)
+    return finish(plan, composition, mixing_rate, cell_index, near, rate_exponents.T, mats)
 
 
 def solution(mesh):

time: 151 us -> 73.2 us (0.48)
  Pallas kernels: 106 us -> 67.1 us
  waiting for transfers between devices: 24.8 us -> 0 us
  between operations: 13.5 us -> 0.11 us
    pallas_call x1, Pallas kernels: 64.1 us -> 24.9 us  [finish(): pl.pallas_call(finish_kernel, out_shape=jax.ShapeDtypeStruct(composition....]
    all_gather x1 -> x0, waiting for transfers between devices: 24.8 us -> none  [local(): mats = lax.all_gather(mat, ('gx', 'yz'), axis=0)]
    unnamed x14 -> x18, local copies, waits for them, and re-layouts: 3.57 us -> 4.03 us
  transfers between devices with their start and end apart: 1 -> 0, of which waited for: 1 -> 0; matrix products, arithmetic and copies ran while one was open for 2% -> 0% of each run, Pallas kernels for 28% -> 0%
where the time goes in v2:
time: 73.2 us; the launch traced here: 72.7 us
  Pallas kernels  67.1 us (92%)
  local copies, waits for them, and re-layouts  5.44 us (7%)
    pallas_call x1, Pallas kernels, exchange(): pl.pallas_call(functools.partial(exchange_kernel, n_gx), out_shape=(jax.S...  29 us
    pallas_call x1, Pallas kernels, finish(): pl.pallas_call(finish_kernel, out_shape=jax.ShapeDtypeStruct(composition....  24.9 us
    pallas_call x1, Pallas kernels, moments(): pl.pallas_call(moments_kernel, out_shape=(jax.ShapeDtypeStruct((2 * HIGHS...  13.3 us
    unnamed x18, local copies, waits for them, and re-layouts  4.03 us

profile of v2, /device:TPU:1, one launch (start us, length us, event | category | flops | bytes accessed | tf_op | source)
XLA Modules:
  0.0 72.7 jit_solution(15343648912519126217)
XLA Ops:
  0.0 0.0 copy-start.1
  0.0 0.0 copy-start.7
  0.0 0.0 copy-start.6
  0.0 0.0 copy-start.3
  0.0 0.8 %copy.22 = f32[1,20,20]{2,1,0:T(8,128)S(1)} copy(f32[1,20,20]{2,0,1:T(1,128)} %param.15) | data formatting | bytes 3200
  0.8 0.1 reshape.7
  0.9 2.1 %copy.14.comp_ref = f32[128,20,128]{2,1,0:T(8,128)S(1)} copy(f32[128,20,128]{2,0,1:T(8,128)} %param.9) | data formatting | bytes 2621440 | tf_op args[0]
  3.0 0.0 copy-done.1
  3.0 0.0 copy-done.7
  3.0 0.0 copy-done.6
  3.0 0.0 copy-done.3
  3.0 0.0 copy-start.4
  3.0 0.0 copy-start.2
  3.1 0.0 copy-start.5
  3.1 13.3 %shard_map.91 = (f32[48,24,128]{2,1,0:T(8,128)S(1)}, s32[8,128]{1,0:T(8,128)S(1)}) custom-call(f32[128,20,128]{2,1,0:T(8,128)S(1)} %copy.14.comp_ref, f32[128,128]{1,0:T(8,128)S(1)} %copy-done.3, s32[128,128]{1,0:T(8,128)S(1)} %copy-done.1, s32[1,128]{1,0:T(1,128)S(1)} %bitcast.9, s32[1,128]{1,0:T(1,128)S(1)} %copy-done.7), custom_call_target="tpu_custom_call" | custom-call | tf_op jit(solution)/shard_map/pallas_call | solution.py:107
  16.3 0.0 copy-done.4
  16.4 29.0 %shard_map.92 = (f32[48,24,128]{2,1,0:T(8,128)S(1)}, f32[128,24,128]{2,1,0:T(8,128)S(1)}) custom-call(f32[48,24,128]{2,1,0:T(8,128)S(1)} %get-tuple-element.10.part_ref, f32[4,128]{1,0:T(4,128)S(1)} %pad.9.packed_ref, f32[20,84]{1,0:T(8,128)S(1)} %copy-done.4), custom_call_target="tpu_custom_call" | custom-call | tf_op jit(solution)/shard_map/pallas_call | solution.py:223
  45.4 0.0 copy-start
  45.4 1.1 %copy-done = f32[128,24,128]{2,1,0:T(8,128)} copy-done((f32[128,24,128]{2,1,0:T(8,128)}, f32[128,24,128]{2,1,0:T(8,128)S(1)}, u32[]{:S(2)}) %copy-start) | copy-done | bytes 1572888
  46.5 0.0 copy-done.2
  46.5 0.0 copy-done.5
  46.5 24.9 %shard_map.93 = f32[128,20,128]{2,1,0:T(8,128)S(1)} custom-call(s32[8,128]{1,0:T(8,128)S(1)} %get-tuple-element.9.plan_ref, f32[128,20,128]{2,1,0:T(8,128)S(1)} %copy.14.comp_ref, f32[128,128]{1,0:T(8,128)S(1)} %copy-done.2, s32[128,128]{1,0:T(8,128)S(1)} %copy-done.1, f32[48,24,128]{2,1,0:T(8,128)S(1)} %get-tuple-element.11.near_ref, f32[20,84]{1,0:T(8,128)S(1)} %bitcast.8, ...), custom_call_target="tpu_custom_call" | custom-call | tf_op jit(solution)/shard_map/pallas_call | solution.py:347
  71.4 1.3 %copy.17 = f32[128,20,128]{2,0,1:T(8,128)} copy(f32[128,20,128]{2,1,0:T(8,128)S(1)} %shard_map.93) | data formatting | bytes 2621440 | tf_op jit(solution)/shard_map/pallas_call | solution.py:347
  (4 shorter events, 0.0 us)
Async XLA Ops:
  0.0 3.0 %copy-start.1 = (s32[128,128]{1,0:T(8,128)S(1)}, s32[128,128]{1,0:T(8,128)}, u32[]{:S(2)}) copy-start(s32[128,128]{1,0:T(8,128)} %cell_ref.3) | copy-start | bytes 196612
  0.0 3.0 %copy-start.7 = (s32[1,128]{1,0:T(1,128)S(1)}, s32[1,128]{1,0:T(1,128)}, u32[]{:S(2)}) copy-start(s32[1,128]{1,0:T(1,128)} %shuffle_ref.1) | copy-start | bytes 1540
  0.0 3.0 %copy-start.6 = (s32[128]{0:T(128)S(1)}, s32[128]{0:T(128)}, u32[]{:S(2)}) copy-start(s32[128]{0:T(128)} %param.13) | copy-start | bytes 1540
  0.0 3.0 %copy-start.3 = (f32[128,128]{1,0:T(8,128)S(1)}, f32[128,128]{1,0:T(8,128)}, u32[]{:S(2)}) copy-start(f32[128,128]{1,0:T(8,128)} %mass_ref.1) | copy-start | bytes 196612
  3.0 13.3 %copy-start.4 = (f32[20,84]{1,0:T(8,128)S(1)}, f32[20,84]{1,0:T(8,128)}, u32[]{:S(2)}) copy-start(f32[20,84]{1,0:T(8,128)} %stoich_ref.1) | copy-start | bytes 20164
  3.0 43.5 %copy-start.2 = (f32[128,128]{1,0:T(8,128)S(1)}, f32[128,128]{1,0:T(8,128)}, u32[]{:S(2)}) copy-start(f32[128,128]{1,0:T(8,128)} %rate_ref.1) | copy-start | bytes 196612
  3.1 43.5 %copy-start.5 = (f32[84,20]{0,1:T(8,128)S(1)}, f32[84,20]{0,1:T(8,128)}, u32[]{:S(2)}) copy-start(f32[84,20]{0,1:T(8,128)} %param.16) | copy-start | bytes 20164
  45.4 1.1 %copy-start = (f32[128,24,128]{2,1,0:T(8,128)}, f32[128,24,128]{2,1,0:T(8,128)S(1)}, u32[]{:S(2)}) copy-start(f32[128,24,128]{2,1,0:T(8,128)S(1)} %get-tuple-element.12.mats_ref) | copy-start | bytes 4718596

commit v3 on v2

v3 whole, which is shorter than its diff:
```python
import functools

import jax
import jax.numpy as jnp
from jax import lax
from jax.experimental import pallas as pl
from jax.experimental.pallas import tpu as pltpu
from jax.sharding import PartitionSpec as P

f32, bf16 = jnp.float32, jnp.bfloat16
MESH = pl.DeviceIdType.MESH
VMEM = pl.BlockSpec(memory_space=pltpu.VMEM)
SMEM = pl.BlockSpec(memory_space=pltpu.SMEM)

NS, NR, LANES = 20, 84, 128
CELL_DEV = 128
COLUMNS = 16
SLAB = CELL_DEV * COLUMNS
LOW = 256
HIGHS = 3 * SLAB // LOW
ROWS = 24
STEPS = 88
TILE = 8
GROUP = 32
STEP_SIZE = 0.25
PACK = 4


def split(x):
    upper = x.astype(bf16)
    return upper, (x - upper.astype(f32)).astype(bf16)


def mm(a, b):
    return jnp.dot(a, b, preferred_element_type=f32)


def gather_kernel(
    n_gx, comp_ref, mass_ref, rate_ref, cell_ref, counts_ref, shuffle_ref, packed_ref, stoich_ref,
    state_ref, mats_ref, plan_ref,
    value_ref, low_ref, spread_ref, acc_ref, pick_ref, table_ref, part_ref, halo_ref, own_ref, sums_ref,
    mine_ref, near_ref, batch_ref, wide_ref,
    halo_send, halo_recv, sum_send, sum_recv, mean_send, mean_recv, left_send, left_recv,
    right_send, right_recv, row_send, row_recv, batch_send, batch_recv,
):
    blocks = mass_ref.shape[0]
    tiles = blocks // TILE
    i, j = lax.axis_index("gx"), lax.axis_index("yz")
    left, right = lax.rem(i + n_gx - 1, n_gx), lax.rem(i + 1, n_gx)
    first = (i - 1) * SLAB
    iota = lax.broadcasted_iota(jnp.int32, (LOW, LANES), 0).astype(f32).astype(bf16)
    one, zero = jnp.ones((), bf16), jnp.zeros((), bf16)
    own_highs = range(HIGHS // 3, 2 * HIGHS // 3)
    other_highs = [h for h in range(HIGHS) if h not in own_highs]

    def column(p):
        return lax.rem(j + p, COLUMNS)

    def gx_peer(p):
        return lax.rem(i + p, n_gx)

    def send(src, dst, send_sem, recv_sem, target):
        copy = pltpu.make_async_remote_copy(
            src_ref=src, dst_ref=dst, send_sem=send_sem, recv_sem=recv_sem,
            device_id=target, device_id_type=MESH,
        )
        copy.start()
        return copy

    barrier = pltpu.get_barrier_semaphore()
    peers = [(gx_peer(p), j) for p in range(1, n_gx)] + [(i, column(p)) for p in range(1, COLUMNS)]
    for target in peers:
        pl.semaphore_signal(barrier, inc=1, device_id=target, device_id_type=MESH)
    batch_ref[j, i] = packed_ref[...]

    def prepare(t):
        base = pl.multiple_of(t * TILE, TILE)
        low = ((cell_ref[pl.ds(base, TILE), :] - first) & (LOW - 1)).astype(f32)
        masses = mass_ref[pl.ds(base, TILE), :]
        for b in range(TILE):
            lanes = slice(b * LANES, (b + 1) * LANES)
            mass = masses[b : b + 1, :]
            value = jnp.concatenate(
                [comp_ref[:, base + b, :] * mass, mass, jnp.zeros((ROWS - NS - 1, LANES), f32)], 0
            )
            upper = value.astype(bf16).astype(f32)
            value_ref[t, :, lanes] = jnp.concatenate([upper, value - upper], 0).astype(bf16)
            low_row = jnp.broadcast_to(low[b : b + 1, :], (LOW, LANES)).astype(bf16)
            low_ref[t, :, lanes] = jnp.where(low_row == iota, one, zero)

    def spread(t, slot, highs):
        base = pl.multiple_of(t * TILE, TILE)
        high = ((cell_ref[pl.ds(base, TILE), :] - first) >> 8).astype(f32)
        for b in range(TILE):
            lanes = slice(b * LANES, (b + 1) * LANES)
            values = value_ref[t, :, lanes]
            high_row = jnp.broadcast_to(high[b : b + 1, :], (2 * ROWS, LANES)).astype(bf16)
            for k, h in enumerate(highs):
                spread_ref[slot, k * 2 * ROWS : (k + 1) * 2 * ROWS, lanes] = jnp.where(
                    high_row == jnp.asarray(h, bf16), values, zero
                )

    def accumulate(t, slot, highs):
        rows = len(highs) * 2 * ROWS
        acc_ref[:rows] += lax.dot_general(
            spread_ref[slot, :rows], low_ref[t], (((1,), (1,)), ((), ())), preferred_element_type=f32
        )

    def owners(highs):
        for k, h in enumerate(highs):
            total = acc_ref[k * 48 : k * 48 + 24, :] + acc_ref[k * 48 + 24 : k * 48 + 48, :]
            yield k, total[:, :CELL_DEV], total[:, CELL_DEV:]

    acc_ref[...] = jnp.zeros_like(acc_ref)

    def other_tiles(u, carry):
        for slot in range(2):
            prepare(2 * u + slot)
            spread(2 * u + slot, slot, other_highs)
            accumulate(2 * u + slot, slot, other_highs)
        return carry

    lax.fori_loop(0, tiles // 2, other_tiles, 0)
    for k, even, odd in owners(other_highs):
        part_ref[2 * k] = even
        part_ref[2 * k + 1] = odd
    acc_ref[...] = jnp.zeros_like(acc_ref)

    pl.semaphore_wait(barrier, len(peers))
    halos = [
        send(part_ref.at[pl.ds(0, COLUMNS)], halo_ref.at[1], halo_send.at[0], halo_recv.at[0], (left, j)),
        send(part_ref.at[pl.ds(COLUMNS, COLUMNS)], halo_ref.at[0], halo_send.at[1], halo_recv.at[1], (right, j)),
    ]
    rows = [
        send(batch_ref.at[j, i], batch_ref.at[j, i], row_send.at[p], row_recv.at[p], (gx_peer(p), j))
        for p in range(1, n_gx)
    ]

    def own_tiles(u, carry):
        for slot in range(2):
            spread(2 * u + slot, slot, own_highs)
            accumulate(2 * u + slot, slot, own_highs)
        return carry

    lax.fori_loop(0, tiles // 4, own_tiles, 0)
    for copy in rows:
        copy.wait()
    batches = [
        send(batch_ref.at[j], batch_ref.at[j], batch_send.at[p], batch_recv.at[p], (i, column(p)))
        for p in range(1, COLUMNS)
    ]
    lax.fori_loop(tiles // 4, tiles // 2, own_tiles, 0)
    for copy in halos:
        copy.wait()
    for k, even, odd in owners(own_highs):
        own_ref[2 * k] = even + halo_ref[0, 2 * k] + halo_ref[1, 2 * k]
        own_ref[2 * k + 1] = odd + halo_ref[0, 2 * k + 1] + halo_ref[1, 2 * k + 1]

    partials = [
        send(own_ref.at[column(p)], sums_ref.at[p], sum_send.at[p], sum_recv.at[p], (i, column(p)))
        for p in range(1, COLUMNS)
    ]

    wide_ref[...] = jnp.zeros_like(wide_ref)
    upper, lower = (v.astype(f32) for v in split(STEP_SIZE * stoich_ref[...]))
    for c in range(NS // PACK):
        lanes = slice(c * LANES, c * LANES + NR)
        for k, piece in enumerate((upper, lower, upper)):
            wide_ref[k * LANES + c * ROWS : k * LANES + c * ROWS + NS, lanes] = piece
    wide = wide_ref[...].astype(bf16)
    for copy in batches:
        copy.wait()
    batch_total = n_gx * COLUMNS
    for t in range(PACK):
        upper, lower = split(batch_ref[:, :, t, :].reshape(batch_total, LANES))
        product = mm(jnp.concatenate([upper, upper, lower], 1), wide)
        for c in range(NS // PACK):
            mats_ref[:, PACK * c + t, :] = product[:, c * LANES : (c + 1) * LANES]
    for r in range(NS, ROWS):
        mats_ref[:, r, :] = jnp.zeros((batch_total, LANES), f32)

    total = own_ref[j]
    for p, copy in enumerate(partials, 1):
        copy.wait()
        total = total + sums_ref[p]
    means = total[:NS] / total[NS : NS + 1]
    mine_ref[...] = jnp.concatenate([means, jnp.zeros((ROWS - NS, CELL_DEV), f32)], 0)

    slab_means = [
        send(mine_ref, near_ref.at[COLUMNS + j], mean_send.at[p], mean_recv.at[p], (i, column(p)))
        for p in range(1, COLUMNS)
    ]
    near_ref[COLUMNS + j] = mine_ref[...]

    def forward(p, src, at):
        return [
            send(src, near_ref.at[2 * COLUMNS + at], left_send.at[p], left_recv.at[p], (left, j)),
            send(src, near_ref.at[at], right_send.at[p], right_recv.at[p], (right, j)),
        ]

    forwards = forward(0, mine_ref, j)

    row = lax.broadcasted_iota(jnp.int32, (blocks, blocks), 0)
    lane = lax.broadcasted_iota(jnp.int32, (blocks, blocks), 1)
    lane_f = lane.astype(f32)
    place = ((row % COLUMNS) * (blocks // COLUMNS) + row // COLUMNS).astype(f32)
    eye = row == lane
    counts = counts_ref[...].astype(f32)
    shuffle = shuffle_ref[...].astype(f32)
    block_of = jnp.sum(jnp.where(eye, shuffle, 0.0), axis=1, keepdims=True)
    count_of = jnp.sum(jnp.where(block_of == lane_f, counts, 0.0), axis=1, keepdims=True)
    count_row = jnp.sum(jnp.where(eye, count_of, 0.0), axis=0, keepdims=True)
    ahead = (count_row > count_of) | ((count_row == count_of) & (lane < row))
    rank = jnp.sum(jnp.where(ahead, 1.0, 0.0), axis=1, keepdims=True)
    here = rank == lane_f
    lines = [jnp.sum(jnp.where(here, v, 0.0), axis=0, keepdims=True) for v in (place, block_of, count_of)]
    plan_ref[...] = jnp.concatenate(lines + [jnp.zeros((5, blocks), f32)], 0).astype(jnp.int32)

    for p, copy in enumerate(slab_means, 1):
        copy.wait()
        source = lax.rem(j - p + COLUMNS, COLUMNS)
        forwards += forward(p, near_ref.at[COLUMNS + source], source)

    def tabulate(highs):
        for k, h in enumerate(highs):
            parts = split(jnp.concatenate([near_ref[2 * h], near_ref[2 * h + 1]], 1))
            for piece in range(2):
                table_ref[piece, k * ROWS : (k + 1) * ROWS] = parts[piece]

    def pick(t, slot, highs):
        rows = len(highs) * ROWS
        pick_ref[slot, :rows] = mm(table_ref[0, :rows], low_ref[t]) + mm(table_ref[1, :rows], low_ref[t])

    def choose(t, slot, highs, b, mean):
        base = pl.multiple_of(t * TILE, TILE)
        high = (cell_ref[pl.ds(base, TILE), :] - first) >> 8
        high_row = jnp.broadcast_to(high[b : b + 1, :], (ROWS, LANES))
        lanes = slice(b * LANES, (b + 1) * LANES)
        for k, h in enumerate(highs):
            mean = jnp.where(high_row == h, pick_ref[slot, k * ROWS : (k + 1) * ROWS, lanes], mean)
        return mean

    tabulate(own_highs)

    def own_lookup(u, carry):
        for slot in range(2):
            t = 2 * u + slot
            pick(t, slot, own_highs)
            for b in range(TILE):
                state_ref[t * TILE + b] = choose(t, slot, own_highs, b, jnp.zeros((ROWS, LANES), f32))
        return carry

    lax.fori_loop(0, tiles // 2, own_lookup, 0)
    for copy in forwards:
        copy.wait()

    tabulate(other_highs)

    def other_lookup(u, carry):
        for slot in range(2):
            t = 2 * u + slot
            base = pl.multiple_of(t * TILE, TILE)
            pick(t, slot, other_highs)
            decay = jnp.exp(-rate_ref[pl.ds(base, TILE), :])
            for b in range(TILE):
                mean = choose(t, slot, other_highs, b, state_ref[base + b])[:NS]
                state_ref[base + b, :NS] = mean + (comp_ref[:, base + b, :] - mean) * decay[b : b + 1, :]
                state_ref[base + b, NS:] = jnp.zeros((ROWS - NS, LANES), f32)
        return carry

    lax.fori_loop(0, tiles // 2, other_lookup, 0)


def gather(n_gx, composition, mass, rate, cell, counts, shuffle, packed, stoichiometry):
    blocks = mass.shape[0]
    dma = pltpu.SemaphoreType.DMA
    piece = (COLUMNS, ROWS, CELL_DEV)
    return pl.pallas_call(
        functools.partial(gather_kernel, n_gx),
        out_shape=(
            jax.ShapeDtypeStruct((blocks, ROWS, LANES), f32),
            jax.ShapeDtypeStruct((n_gx * COLUMNS, ROWS, LANES), f32),
            jax.ShapeDtypeStruct((8, blocks), jnp.int32),
        ),
        in_specs=[VMEM] * 8,
        out_specs=(VMEM,) * 3,
        scratch_shapes=[
            pltpu.VMEM((blocks // TILE, 2 * ROWS, TILE * LANES), bf16),
            pltpu.VMEM((blocks // TILE, LOW, TILE * LANES), bf16),
            pltpu.VMEM((2, HIGHS * 2 * ROWS * 2 // 3, TILE * LANES), bf16),
            pltpu.VMEM((HIGHS * 2 * ROWS * 2 // 3, LOW), f32),
            pltpu.VMEM((2, HIGHS * ROWS * 2 // 3, TILE * LANES), f32),
            pltpu.VMEM((2, HIGHS * ROWS * 2 // 3, LOW), bf16),
            pltpu.VMEM((2 * COLUMNS, ROWS, CELL_DEV), f32),
            pltpu.VMEM((2, *piece), f32),
            pltpu.VMEM(piece, f32),
            pltpu.VMEM(piece, f32),
            pltpu.VMEM((ROWS, CELL_DEV), f32),
            pltpu.VMEM((3 * COLUMNS, ROWS, CELL_DEV), f32),
            pltpu.VMEM((COLUMNS, n_gx, PACK, LANES), f32),
            pltpu.VMEM((3 * LANES, NS // PACK * LANES), f32),
            dma((2,)), dma((2,)), *[dma((COLUMNS,))] * 8,
            dma((n_gx,)), dma((n_gx,)), dma((COLUMNS,)), dma((COLUMNS,)),
        ],
        compiler_params=pltpu.CompilerParams(
            collective_id=0, has_side_effects=True, vmem_limit_bytes=48 << 20
        ),
    )(composition, mass, rate, cell, counts, shuffle, packed, stoichiometry)


def react_kernel(plan_ref, state_ref, rates_ref, mats_ref, out_ref, pair_ref, turn_ref):
    blocks = state_ref.shape[0]
    turn_ref[...] = jnp.zeros_like(turn_ref)
    upper, lower = (v.astype(f32) for v in split(rates_ref[...]))
    for k, piece in enumerate((upper, upper, lower)):
        turn_ref[k * ROWS : k * ROWS + NS, :NR] = piece
    rates = turn_ref[...].T[:STEPS, : 3 * ROWS].astype(bf16)
    lane = lax.broadcasted_iota(jnp.int32, (ROWS, LANES), 1)

    def group(g, carry):
        at = [g * GROUP + b for b in range(GROUP)]
        block = [plan_ref[1, a] for a in at]
        need = [plan_ref[2, a] for a in at]
        for b in range(GROUP):
            upper, lower = (v.astype(f32) for v in split(mats_ref[plan_ref[0, at[b]]]))
            turned = pltpu.roll(upper, STEPS, 1)
            head = jnp.where(lane < STEPS, upper, turned)
            tail = jnp.where(lane < 2 * STEPS - LANES, turned, 0.0)
            pair_ref[b, :, :LANES] = jnp.concatenate([head, lower], 0).astype(bf16)
            pair_ref[b, :, LANES:] = jnp.concatenate([tail, jnp.zeros((ROWS, LANES), f32)], 0).astype(bf16)

        def section(s, states):
            x = jnp.concatenate(states, 1)
            upper = x.astype(bf16).astype(f32)
            progress = jnp.tanh(mm(rates, jnp.concatenate([upper, x - upper, upper], 0).astype(bf16)))
            upper = progress.astype(bf16).astype(f32)
            progress = jnp.concatenate([upper, progress - upper], 0).astype(bf16)
            products = [
                mm(
                    pair_ref[b : b + 2].reshape(4 * ROWS, 2 * LANES)[:, : 2 * STEPS],
                    progress[:, b * LANES : (b + 2) * LANES],
                )
                for b in range(0, GROUP, 2)
            ]
            after = []
            for b, y in zip(range(0, GROUP, 2), products):
                first_change = y[:24, :LANES] + y[24:48, :LANES]
                second_change = y[48:72, LANES:] + y[72:, LANES:]
                after.append(jnp.where(s < need[b], states[b] + first_change, states[b]))
                after.append(jnp.where(s < need[b + 1], states[b + 1] + second_change, states[b + 1]))
            return tuple(after)

        states = lax.fori_loop(0, need[0], section, tuple(state_ref[b] for b in block))
        for b in range(GROUP):
            out_ref[:, block[b], :] = states[b][:NS]
        return carry

    lax.fori_loop(0, blocks // GROUP, group, 0)


def react(plan, state, rates, mats):
    blocks = state.shape[0]
    return pl.pallas_call(
        react_kernel,
        out_shape=jax.ShapeDtypeStruct((NS, blocks, LANES), f32),
        in_specs=[SMEM] + [VMEM] * 3,
        out_specs=VMEM,
        scratch_shapes=[
            pltpu.VMEM((GROUP, 2 * ROWS, 2 * LANES), bf16),
            pltpu.VMEM((LANES, LANES), f32),
        ],
        compiler_params=pltpu.CompilerParams(vmem_limit_bytes=30 << 20),
    )(plan, state, rates, mats)


def local(
    n_gx, composition, particle_mass, mixing_rate, cell_index, section_counts,
    block_shuffle, batch_inverse, rate_exponents, stoichiometry,
):
    packed = jnp.pad(batch_inverse[0], ((0, 0), (0, ROWS - NS)))
    packed = packed.reshape(NS // PACK, PACK, ROWS).transpose(1, 0, 2).reshape(PACK, NS // PACK * ROWS)
    packed = jnp.pad(packed, ((0, 0), (0, LANES - NS // PACK * ROWS)))
    state, mats, plan = gather(
        n_gx, composition.transpose(1, 0, 2), particle_mass, mixing_rate, cell_index,
        section_counts[None], block_shuffle, packed, stoichiometry,
    )
    return react(plan, state, rate_exponents.T, mats).transpose(1, 0, 2)


def solution(mesh):
    both = ("gx", "yz")
    in_specs = (
        P(both, None, None), P(both, None), P(both, None), P(both, None), P(both),
        P(both, None), P(both, None, None), P(), P(),
    )
    return jax.shard_map(
        functools.partial(local, mesh.shape["gx"]),
        mesh=mesh, in_specs=in_specs, out_specs=P(both, None, None), check_vma=False,
    )
```

time: 73.2 us -> 69.3 us (0.947)
  the two profiles are of different devices: /device:TPU:1 before, /device:TPU:0 now
where the time goes in v3:
time: 69.3 us; the launch traced here: 68.9 us
  Pallas kernels  62.2 us (90%)
  local copies, waits for them, and re-layouts  6.69 us (10%)
    pallas_call x1, Pallas kernels, gather(): pl.pallas_call(functools.partial(gather_kernel, n_gx), out_shape=(jax.Sha...  47.9 us
    pallas_call x1, Pallas kernels, react(): pl.pallas_call(react_kernel, out_shape=jax.ShapeDtypeStruct((NS, blocks,...  14.3 us
    unnamed x17, local copies, waits for them, and re-layouts  6.57 us

profile of v3, /device:TPU:0, one launch (start us, length us, event | category | flops | bytes accessed | tf_op | source)
XLA Modules:
  0.0 68.9 jit_solution(653084294857263829)
XLA Ops:
  0.0 0.0 copy-start.5
  0.0 0.7 %copy.16 = f32[1,20,20]{2,1,0:T(8,128)S(1)} copy(f32[1,20,20]{2,0,1:T(1,128)} %param.15) | data formatting | bytes 3200
  0.7 0.1 reshape.7
  0.8 0.0 copy-start
  0.8 1.3 %copy-done = f32[128,20,128]{2,0,1:T(8,128)S(1)} copy-done((f32[128,20,128]{2,0,1:T(8,128)S(1)}, f32[128,20,128]{2,0,1:T(8,128)}, u32[]{:S(2)}) %copy-start) | copy-done | bytes 1310744
  2.2 0.0 copy-start.1
  2.2 0.8 %copy-done.1 = f32[128,128]{1,0:T(8,128)S(1)} copy-done((f32[128,128]{1,0:T(8,128)S(1)}, f32[128,128]{1,0:T(8,128)}, u32[]{:S(2)}) %copy-start.1) | copy-done | bytes 65560
  3.0 0.0 copy-start.2
  3.0 0.8 %copy-done.2 = f32[128,128]{1,0:T(8,128)S(1)} copy-done((f32[128,128]{1,0:T(8,128)S(1)}, f32[128,128]{1,0:T(8,128)}, u32[]{:S(2)}) %copy-start.2) | copy-done | bytes 65560
  3.8 0.0 copy-start.3
  3.8 0.8 %copy-done.3 = s32[128,128]{1,0:T(8,128)S(1)} copy-done((s32[128,128]{1,0:T(8,128)S(1)}, s32[128,128]{1,0:T(8,128)}, u32[]{:S(2)}) %copy-start.3) | copy-done | bytes 65560
  4.7 0.0 copy-start.4
  4.7 0.7 %copy-done.4 = f32[20,84]{1,0:T(8,128)S(1)} copy-done((f32[20,84]{1,0:T(8,128)S(1)}, f32[20,84]{1,0:T(8,128)}, u32[]{:S(2)}) %copy-start.4) | copy-done | bytes 6744
  5.4 0.0 copy-start.6
  5.4 0.7 copy-done.6
  6.0 0.0 copy-start.7
  6.0 0.7 copy-done.7
  6.7 47.9 %shard_map.91 = (f32[128,24,128]{2,1,0:T(8,128)S(1)}, f32[128,24,128]{2,1,0:T(8,128)S(1)}, s32[8,128]{1,0:T(8,128)S(1)}) custom-call(f32[20,128,128]{2,1,0:T(8,128)S(1)} %bitcast.10, f32[128,128]{1,0:T(8,128)S(1)} %copy-done.1, f32[128,128]{1,0:T(8,128)S(1)} %copy-done.2, s32[128,128]{1,0:T(8,128)S(1)} %copy-done.3, s32[1,128]{1,0:T(1,128)S(1)} %bitcast.12, ...), custom_call_target="tpu_custom_call" | custom-call | tf_op jit(solution)/shard_map/pallas_call | solution.py:278
  54.6 0.0 copy-done.5
  54.6 14.3 %shard_map.92 = f32[20,128,128]{2,1,0:T(8,128)} custom-call(s32[8,128]{1,0:T(8,128)S(1)} %get-tuple-element.8.plan_ref, f32[128,24,128]{2,1,0:T(8,128)S(1)} %get-tuple-element.9.state_ref, f32[20,84]{1,0:T(8,128)S(1)} %bitcast.11, f32[128,24,128]{2,1,0:T(8,128)S(1)} %get-tuple-element.10.mats_ref), custom_call_target="tpu_custom_call" | custom-call | tf_op jit(solution)/shard_map/pallas_call | solution.py:363
  (4 shorter events, 0.0 us)
Async XLA Ops:
  0.0 54.6 %copy-start.5 = (f32[84,20]{0,1:T(8,128)S(1)}, f32[84,20]{0,1:T(8,128)}, u32[]{:S(2)}) copy-start(f32[84,20]{0,1:T(8,128)} %param.16) | copy-start | bytes 20164
  0.8 1.3 %copy-start = (f32[128,20,128]{2,0,1:T(8,128)S(1)}, f32[128,20,128]{2,0,1:T(8,128)}, u32[]{:S(2)}) copy-start(f32[128,20,128]{2,0,1:T(8,128)} %param.9) | copy-start | bytes 3932164
  2.2 0.8 %copy-start.1 = (f32[128,128]{1,0:T(8,128)S(1)}, f32[128,128]{1,0:T(8,128)}, u32[]{:S(2)}) copy-start(f32[128,128]{1,0:T(8,128)} %mass_ref.1) | copy-start | bytes 196612
  3.0 0.8 %copy-start.2 = (f32[128,128]{1,0:T(8,128)S(1)}, f32[128,128]{1,0:T(8,128)}, u32[]{:S(2)}) copy-start(f32[128,128]{1,0:T(8,128)} %rate_ref.1) | copy-start | bytes 196612
  3.8 0.8 %copy-start.3 = (s32[128,128]{1,0:T(8,128)S(1)}, s32[128,128]{1,0:T(8,128)}, u32[]{:S(2)}) copy-start(s32[128,128]{1,0:T(8,128)} %cell_ref.1) | copy-start | bytes 196612
  4.7 0.7 %copy-start.4 = (f32[20,84]{1,0:T(8,128)S(1)}, f32[20,84]{1,0:T(8,128)}, u32[]{:S(2)}) copy-start(f32[20,84]{1,0:T(8,128)} %stoich_ref.1) | copy-start | bytes 20164
  5.4 0.7 copy-start.6
  6.0 0.7 copy-start.7

commit v4 on v3

--- a/solution.py
+++ b/solution.py
@@ -11,6 +11,7 @@
 MESH = pl.DeviceIdType.MESH
 VMEM = pl.BlockSpec(memory_space=pltpu.VMEM)
 SMEM = pl.BlockSpec(memory_space=pltpu.SMEM)
+HBM = pl.BlockSpec(memory_space=pltpu.HBM)
 
 NS, NR, LANES = 20, 84, 128
 CELL_DEV = 128
@@ -36,13 +37,24 @@
 
 
 def gather_kernel(
-    n_gx, comp_ref, mass_ref, rate_ref, cell_ref, counts_ref, shuffle_ref, packed_ref, stoich_ref,
-    state_ref, mats_ref, plan_ref,
-    value_ref, low_ref, spread_ref, acc_ref, pick_ref, table_ref, part_ref, halo_ref, own_ref, sums_ref,
-    mine_ref, near_ref, batch_ref, wide_ref,
-    halo_send, halo_recv, sum_send, sum_recv, mean_send, mean_recv, left_send, left_recv,
-    right_send, right_recv, row_send, row_recv, batch_send, batch_recv,
+    n_gx, *refs,
 ):
+    args, refs = refs[:8], refs[8:]
+    outs = refs[:3]
+    comp_ref, mass_ref, rate_ref, cell_ref, counts_ref, shuffle_ref, inverse_ref, stoich_ref = refs[3:11]
+    (
+        state_ref, mats_ref, plan_ref, fetch_sem, store_sem, square_ref,
+        value_ref, low_ref, spread_ref, acc_ref, pick_ref, table_ref, part_ref, halo_ref, own_ref, sums_ref,
+        mine_ref, near_ref, batch_ref, wide_ref,
+        halo_send, halo_recv, sum_send, sum_recv, mean_send, mean_recv, left_send, left_recv,
+        right_send, right_recv, row_send, row_recv, batch_send, batch_recv,
+    ) = refs[11:]
+    fetches = [
+        pltpu.make_async_copy(src, dst, fetch_sem.at[k])
+        for k, (src, dst) in enumerate(zip(args, refs[3:11]))
+    ]
+    for copy in fetches:
+        copy.start()
     blocks = mass_ref.shape[0]
     tiles = blocks // TILE
     i, j = lax.axis_index("gx"), lax.axis_index("yz")
@@ -71,7 +83,16 @@
     peers = [(gx_peer(p), j) for p in range(1, n_gx)] + [(i, column(p)) for p in range(1, COLUMNS)]
     for target in peers:
         pl.semaphore_signal(barrier, inc=1, device_id=target, device_id_type=MESH)
-    batch_ref[j, i] = packed_ref[...]
+    acc_ref[...] = jnp.zeros_like(acc_ref)
+    square_ref[...] = jnp.zeros_like(square_ref)
+    for copy in fetches:
+        copy.wait()
+
+    square_ref[:NS, :NS] = inverse_ref[:, 0, :]
+    packed = square_ref[:PACK]
+    for c in range(1, NS // PACK):
+        packed = packed + pltpu.roll(square_ref[PACK * c : PACK * (c + 1)], c * ROWS, 1)
+    batch_ref[j, i] = packed
 
     def prepare(t):
         base = pl.multiple_of(t * TILE, TILE)
@@ -111,7 +132,6 @@
             total = acc_ref[k * 48 : k * 48 + 24, :] + acc_ref[k * 48 + 24 : k * 48 + 48, :]
             yield k, total[:, :CELL_DEV], total[:, CELL_DEV:]
 
-    acc_ref[...] = jnp.zeros_like(acc_ref)
 
     def other_tiles(u, carry):
         for slot in range(2):
@@ -178,6 +198,8 @@
             mats_ref[:, PACK * c + t, :] = product[:, c * LANES : (c + 1) * LANES]
     for r in range(NS, ROWS):
         mats_ref[:, r, :] = jnp.zeros((batch_total, LANES), f32)
+    stores = [pltpu.make_async_copy(mats_ref, outs[1], store_sem.at[tiles // 2])]
+    stores[0].start()
 
     total = own_ref[j]
     for p, copy in enumerate(partials, 1):
@@ -215,6 +237,8 @@
     here = rank == lane_f
     lines = [jnp.sum(jnp.where(here, v, 0.0), axis=0, keepdims=True) for v in (place, block_of, count_of)]
     plan_ref[...] = jnp.concatenate(lines + [jnp.zeros((5, blocks), f32)], 0).astype(jnp.int32)
+    stores.append(pltpu.make_async_copy(plan_ref, outs[2], store_sem.at[tiles // 2 + 1]))
+    stores[1].start()
 
     for p, copy in enumerate(slab_means, 1):
         copy.wait()
@@ -266,25 +290,39 @@
                 mean = choose(t, slot, other_highs, b, state_ref[base + b])[:NS]
                 state_ref[base + b, :NS] = mean + (comp_ref[:, base + b, :] - mean) * decay[b : b + 1, :]
                 state_ref[base + b, NS:] = jnp.zeros((ROWS - NS, LANES), f32)
+        store_state(u).start()
         return carry
 
+    def store_state(u):
+        part = pl.ds(pl.multiple_of(u * 2 * TILE, 2 * TILE), 2 * TILE)
+        return pltpu.make_async_copy(state_ref.at[part], outs[0].at[part], store_sem.at[u])
+
     lax.fori_loop(0, tiles // 2, other_lookup, 0)
-
-
-def gather(n_gx, composition, mass, rate, cell, counts, shuffle, packed, stoichiometry):
-    blocks = mass.shape[0]
+    for copy in stores:
+        copy.wait()
+    for u in range(tiles // 2):
+        store_state(u).wait()
+
+
+def gather(n_gx, *args):
+    blocks = args[1].shape[0]
     dma = pltpu.SemaphoreType.DMA
     piece = (COLUMNS, ROWS, CELL_DEV)
+    outs = (
+        jax.ShapeDtypeStruct((blocks, ROWS, LANES), f32),
+        jax.ShapeDtypeStruct((n_gx * COLUMNS, ROWS, LANES), f32),
+        jax.ShapeDtypeStruct((8, blocks), jnp.int32),
+    )
     return pl.pallas_call(
         functools.partial(gather_kernel, n_gx),
-        out_shape=(
-            jax.ShapeDtypeStruct((blocks, ROWS, LANES), f32),
-            jax.ShapeDtypeStruct((n_gx * COLUMNS, ROWS, LANES), f32),
-            jax.ShapeDtypeStruct((8, blocks), jnp.int32),
-        ),
-        in_specs=[VMEM] * 8,
-        out_specs=(VMEM,) * 3,
+        out_shape=outs,
+        in_specs=[HBM] * 8,
+        out_specs=(HBM,) * 3,
         scratch_shapes=[
+            *[pltpu.VMEM(a.shape, a.dtype) for a in (*args, *outs)],
+            dma((len(args),)),
+            dma((blocks // TILE // 2 + 2,)),
+            pltpu.VMEM((ROWS, LANES), f32),
             pltpu.VMEM((blocks // TILE, 2 * ROWS, TILE * LANES), bf16),
             pltpu.VMEM((blocks // TILE, LOW, TILE * LANES), bf16),
             pltpu.VMEM((2, HIGHS * 2 * ROWS * 2 // 3, TILE * LANES), bf16),
@@ -303,19 +341,29 @@
             dma((n_gx,)), dma((n_gx,)), dma((COLUMNS,)), dma((COLUMNS,)),
         ],
         compiler_params=pltpu.CompilerParams(
-            collective_id=0, has_side_effects=True, vmem_limit_bytes=48 << 20
+            collective_id=0, has_side_effects=True, vmem_limit_bytes=60 << 20
         ),
-    )(composition, mass, rate, cell, counts, shuffle, packed, stoichiometry)
-
-
-def react_kernel(plan_ref, state_ref, rates_ref, mats_ref, out_ref, pair_ref, turn_ref):
+    )(*args)
+
+
+def react_kernel(plan_ref, *refs):
+    args, (out_ref, state_ref, rates_ref, mats_ref, fetch_sem, pair_ref, turn_ref) = refs[:3], refs[3:]
+    fetches = [
+        pltpu.make_async_copy(src, dst, fetch_sem.at[k])
+        for k, (src, dst) in enumerate(zip(args, (state_ref, rates_ref, mats_ref)))
+    ]
+    for copy in fetches:
+        copy.start()
     blocks = state_ref.shape[0]
+    fetches[1].wait()
     turn_ref[...] = jnp.zeros_like(turn_ref)
     upper, lower = (v.astype(f32) for v in split(rates_ref[...]))
     for k, piece in enumerate((upper, upper, lower)):
         turn_ref[k * ROWS : k * ROWS + NS, :NR] = piece
     rates = turn_ref[...].T[:STEPS, : 3 * ROWS].astype(bf16)
     lane = lax.broadcasted_iota(jnp.int32, (ROWS, LANES), 1)
+    fetches[0].wait()
+    fetches[2].wait()
 
     def group(g, carry):
         at = [g * GROUP + b for b in range(GROUP)]
@@ -363,13 +411,15 @@
     return pl.pallas_call(
         react_kernel,
         out_shape=jax.ShapeDtypeStruct((NS, blocks, LANES), f32),
-        in_specs=[SMEM] + [VMEM] * 3,
+        in_specs=[SMEM] + [HBM] * 3,
         out_specs=VMEM,
         scratch_shapes=[
+            *[pltpu.VMEM(a.shape, a.dtype) for a in (state, rates, mats)],
+            pltpu.SemaphoreType.DMA((3,)),
             pltpu.VMEM((GROUP, 2 * ROWS, 2 * LANES), bf16),
             pltpu.VMEM((LANES, LANES), f32),
         ],
-        compiler_params=pltpu.CompilerParams(vmem_limit_bytes=30 << 20),
+        compiler_params=pltpu.CompilerParams(vmem_limit_bytes=60 << 20),
     )(plan, state, rates, mats)
 
 
@@ -377,12 +427,9 @@
     n_gx, composition, particle_mass, mixing_rate, cell_index, section_counts,
     block_shuffle, batch_inverse, rate_exponents, stoichiometry,
 ):
-    packed = jnp.pad(batch_inverse[0], ((0, 0), (0, ROWS - NS)))
-    packed = packed.reshape(NS // PACK, PACK, ROWS).transpose(1, 0, 2).reshape(PACK, NS // PACK * ROWS)
-    packed = jnp.pad(packed, ((0, 0), (0, LANES - NS // PACK * ROWS)))
     state, mats, plan = gather(
         n_gx, composition.transpose(1, 0, 2), particle_mass, mixing_rate, cell_index,
-        section_counts[None], block_shuffle, packed, stoichiometry,
+        section_counts[None], block_shuffle, batch_inverse.transpose(1, 0, 2), stoichiometry,
     )
     return react(plan, state, rate_exponents.T, mats).transpose(1, 0, 2)
 

time: 69.3 us -> 66.7 us (0.962)
  the two profiles are of different devices: /device:TPU:0 before, /device:TPU:1 now
where the time goes in v4:
time: 66.7 us; the launch traced here: 66.5 us
  Pallas kernels  66.5 us (100%)
    pallas_call x1, Pallas kernels, gather(): pl.pallas_call(functools.partial(gather_kernel, n_gx), out_shape=outs, in...  50.2 us
    pallas_call x1, Pallas kernels, react(): pl.pallas_call(react_kernel, out_shape=jax.ShapeDtypeStruct((NS, blocks,...  16.3 us

profile of v4, /device:TPU:1, one launch (start us, length us, event | category | flops | bytes accessed | tf_op | source)
XLA Modules:
  0.0 66.5 jit_solution(14739048648530303308)
XLA Ops:
  0.0 50.2 %shard_map.91 = (f32[128,24,128]{2,1,0:T(8,128)}, f32[128,24,128]{2,1,0:T(8,128)}, s32[8,128]{1,0:T(8,128)}) custom-call(f32[20,128,128]{2,1,0:T(8,128)} %bitcast.5, f32[128,128]{1,0:T(8,128)} %refs_1_.1, f32[128,128]{1,0:T(8,128)} %refs_2_.1, s32[128,128]{1,0:T(8,128)} %refs_3_.1, s32[1,128]{1,0:T(1,128)} %bitcast.8, s32[1,128]{1,0:T(1,128)} %refs_5_.1, ...), custom_call_target="tpu_custom_call" | custom-call | tf_op jit(solution)/shard_map/pallas_call | solution.py:316
  50.2 16.3 %shard_map.92 = f32[20,128,128]{2,1,0:T(8,128)} custom-call(s32[8,128]{1,0:T(8,128)} %get-tuple-element.8.plan_ref, f32[128,24,128]{2,1,0:T(8,128)} %get-tuple-element.9.refs_0_, f32[20,84]{1,0:T(8,128)} %bitcast.6, f32[128,24,128]{2,1,0:T(8,128)} %get-tuple-element.10.refs_2_), custom_call_target="tpu_custom_call" | custom-call | tf_op jit(solution)/shard_map/pallas_call | solution.py:411

commit v5 on v4

--- a/solution.py
+++ b/solution.py
@@ -7,7 +7,7 @@
 from jax.experimental.pallas import tpu as pltpu
 from jax.sharding import PartitionSpec as P
 
-f32, bf16 = jnp.float32, jnp.bfloat16
+f32, bf16, f8 = jnp.float32, jnp.bfloat16, jnp.float8_e4m3fn
 MESH = pl.DeviceIdType.MESH
 VMEM = pl.BlockSpec(memory_space=pltpu.VMEM)
 SMEM = pl.BlockSpec(memory_space=pltpu.SMEM)
@@ -22,14 +22,23 @@
 ROWS = 24
 STEPS = 88
 TILE = 8
-GROUP = 32
+GROUP = 16
 STEP_SIZE = 0.25
+PARTS = 64
+TOP = 224.0
+MASS_SCALE = 64.0
 PACK = 4
 
 
 def split(x):
     upper = x.astype(bf16)
     return upper, (x - upper.astype(f32)).astype(bf16)
+
+
+def cut(x):
+    first = x.astype(f8).astype(f32)
+    second = (x - first).astype(f8).astype(f32)
+    return first, second, x - first - second
 
 
 def mm(a, b):
@@ -44,8 +53,8 @@
     comp_ref, mass_ref, rate_ref, cell_ref, counts_ref, shuffle_ref, inverse_ref, stoich_ref = refs[3:11]
     (
         state_ref, mats_ref, plan_ref, fetch_sem, store_sem, square_ref,
-        value_ref, low_ref, spread_ref, acc_ref, pick_ref, table_ref, part_ref, halo_ref, own_ref, sums_ref,
-        mine_ref, near_ref, batch_ref, wide_ref,
+        value_ref, low_ref, spread_ref, acc_ref, pick_ref, table_ref, wide_table_ref, part_ref, halo_ref, own_ref, sums_ref,
+        mine_ref, near_ref, batch_ref, wide_ref, product_ref,
         halo_send, halo_recv, sum_send, sum_recv, mean_send, mean_recv, left_send, left_recv,
         right_send, right_recv, row_send, row_recv, batch_send, batch_recv,
     ) = refs[11:]
@@ -94,6 +103,10 @@
         packed = packed + pltpu.roll(square_ref[PACK * c : PACK * (c + 1)], c * ROWS, 1)
     batch_ref[j, i] = packed
 
+    bound = jnp.max(jnp.abs(comp_ref[...]), keepdims=True).reshape(1, 1) * jnp.max(mass_ref[...], keepdims=True)
+    bound = jnp.maximum(bound, 1e-30)
+    scale, unscale = TOP / bound, bound / TOP
+
     def prepare(t):
         base = pl.multiple_of(t * TILE, TILE)
         low = ((cell_ref[pl.ds(base, TILE), :] - first) & (LOW - 1)).astype(f32)
@@ -101,13 +114,13 @@
         for b in range(TILE):
             lanes = slice(b * LANES, (b + 1) * LANES)
             mass = masses[b : b + 1, :]
-            value = jnp.concatenate(
-                [comp_ref[:, base + b, :] * mass, mass, jnp.zeros((ROWS - NS - 1, LANES), f32)], 0
-            )
-            upper = value.astype(bf16).astype(f32)
-            value_ref[t, :, lanes] = jnp.concatenate([upper, value - upper], 0).astype(bf16)
+            value = cut(comp_ref[:, base + b, :] * (mass * scale))
+            weight = cut(mass * MASS_SCALE)
+            value_ref[t, :, lanes] = jnp.concatenate(
+                [value[0], *weight, jnp.zeros((1, LANES), f32), value[1], value[2]], 0
+            ).astype(bf16)
             low_row = jnp.broadcast_to(low[b : b + 1, :], (LOW, LANES)).astype(bf16)
-            low_ref[t, :, lanes] = jnp.where(low_row == iota, one, zero)
+            low_ref[t, :, lanes] = jnp.where(low_row == iota, one, zero).astype(f8)
 
     def spread(t, slot, highs):
         base = pl.multiple_of(t * TILE, TILE)
@@ -115,21 +128,24 @@
         for b in range(TILE):
             lanes = slice(b * LANES, (b + 1) * LANES)
             values = value_ref[t, :, lanes]
-            high_row = jnp.broadcast_to(high[b : b + 1, :], (2 * ROWS, LANES)).astype(bf16)
+            high_row = jnp.broadcast_to(high[b : b + 1, :], (PARTS, LANES)).astype(bf16)
             for k, h in enumerate(highs):
-                spread_ref[slot, k * 2 * ROWS : (k + 1) * 2 * ROWS, lanes] = jnp.where(
+                spread_ref[slot, k * PARTS : (k + 1) * PARTS, lanes] = jnp.where(
                     high_row == jnp.asarray(h, bf16), values, zero
-                )
+                ).astype(f8)
 
     def accumulate(t, slot, highs):
-        rows = len(highs) * 2 * ROWS
+        rows = len(highs) * PARTS
         acc_ref[:rows] += lax.dot_general(
             spread_ref[slot, :rows], low_ref[t], (((1,), (1,)), ((), ())), preferred_element_type=f32
         )
 
     def owners(highs):
         for k, h in enumerate(highs):
-            total = acc_ref[k * 48 : k * 48 + 24, :] + acc_ref[k * 48 + 24 : k * 48 + 48, :]
+            sums = acc_ref[k * PARTS : (k + 1) * PARTS, :]
+            value = (sums[:NS] + sums[ROWS : ROWS + NS] + sums[ROWS + NS :]) * unscale
+            weight = (sums[NS : NS + 1] + sums[NS + 1 : NS + 2] + sums[NS + 2 : NS + 3]) * (1 / MASS_SCALE)
+            total = jnp.concatenate([value, weight, jnp.zeros((ROWS - NS - 1, LOW), f32)], 0)
             yield k, total[:, :CELL_DEV], total[:, CELL_DEV:]
 
 
@@ -184,9 +200,10 @@
     wide_ref[...] = jnp.zeros_like(wide_ref)
     upper, lower = (v.astype(f32) for v in split(STEP_SIZE * stoich_ref[...]))
     for c in range(NS // PACK):
-        lanes = slice(c * LANES, c * LANES + NR)
         for k, piece in enumerate((upper, lower, upper)):
-            wide_ref[k * LANES + c * ROWS : k * LANES + c * ROWS + NS, lanes] = piece
+            for start in (0, STEPS):
+                lanes = slice(2 * c * LANES + start, 2 * c * LANES + start + NR)
+                wide_ref[k * LANES + c * ROWS : k * LANES + c * ROWS + NS, lanes] = piece
     wide = wide_ref[...].astype(bf16)
     for copy in batches:
         copy.wait()
@@ -195,9 +212,21 @@
         upper, lower = split(batch_ref[:, :, t, :].reshape(batch_total, LANES))
         product = mm(jnp.concatenate([upper, upper, lower], 1), wide)
         for c in range(NS // PACK):
-            mats_ref[:, PACK * c + t, :] = product[:, c * LANES : (c + 1) * LANES]
+            for side in range(2):
+                at = (2 * c + side) * LANES
+                product_ref[:, PACK * c + t, side * LANES : (side + 1) * LANES] = product[:, at : at + LANES]
     for r in range(NS, ROWS):
-        mats_ref[:, r, :] = jnp.zeros((batch_total, LANES), f32)
+        product_ref[:, r, :] = jnp.zeros((batch_total, 2 * LANES), f32)
+    once = lax.broadcasted_iota(jnp.int32, (ROWS, 2 * LANES), 1) < STEPS
+
+    def pair(u, carry):
+        for k in range(8):
+            value = product_ref[8 * u + k]
+            upper = value.astype(bf16).astype(f32)
+            mats_ref[8 * u + k] = jnp.concatenate([upper, jnp.where(once, value - upper, 0.0)], 0).astype(bf16)
+        return carry
+
+    lax.fori_loop(0, batch_total // 8, pair, 0)
     stores = [pltpu.make_async_copy(mats_ref, outs[1], store_sem.at[tiles // 2])]
     stores[0].start()
 
@@ -246,39 +275,47 @@
         forwards += forward(p, near_ref.at[COLUMNS + source], source)
 
     def tabulate(highs):
+        bound = jnp.zeros((ROWS, CELL_DEV), f32)
+        for h in highs:
+            bound = jnp.maximum(bound, jnp.maximum(jnp.abs(near_ref[2 * h]), jnp.abs(near_ref[2 * h + 1])))
+        bound = jnp.maximum(jnp.max(bound, keepdims=True), 1e-30)
         for k, h in enumerate(highs):
-            parts = split(jnp.concatenate([near_ref[2 * h], near_ref[2 * h + 1]], 1))
-            for piece in range(2):
-                table_ref[piece, k * ROWS : (k + 1) * ROWS] = parts[piece]
+            parts = cut(jnp.concatenate([near_ref[2 * h], near_ref[2 * h + 1]], 1) * (TOP / bound))
+            for piece in range(3):
+                wide_table_ref[piece, k * ROWS : (k + 1) * ROWS] = parts[piece]
+        rows = len(highs) * ROWS
+        table_ref[:, :rows] = wide_table_ref[:, :rows].astype(f8)
+        return bound / TOP
 
     def pick(t, slot, highs):
         rows = len(highs) * ROWS
-        pick_ref[slot, :rows] = mm(table_ref[0, :rows], low_ref[t]) + mm(table_ref[1, :rows], low_ref[t])
-
-    def choose(t, slot, highs, b, mean):
+        pick_ref[slot, :rows] = sum(mm(table_ref[piece, :rows], low_ref[t]) for piece in range(3))
+
+    def choose(t, slot, highs, b):
         base = pl.multiple_of(t * TILE, TILE)
         high = (cell_ref[pl.ds(base, TILE), :] - first) >> 8
         high_row = jnp.broadcast_to(high[b : b + 1, :], (ROWS, LANES))
         lanes = slice(b * LANES, (b + 1) * LANES)
+        mean = jnp.zeros((ROWS, LANES), f32)
         for k, h in enumerate(highs):
             mean = jnp.where(high_row == h, pick_ref[slot, k * ROWS : (k + 1) * ROWS, lanes], mean)
         return mean
 
-    tabulate(own_highs)
+    own_unscale = tabulate(own_highs)
 
     def own_lookup(u, carry):
         for slot in range(2):
             t = 2 * u + slot
             pick(t, slot, own_highs)
             for b in range(TILE):
-                state_ref[t * TILE + b] = choose(t, slot, own_highs, b, jnp.zeros((ROWS, LANES), f32))
+                state_ref[t * TILE + b] = choose(t, slot, own_highs, b) * own_unscale
         return carry
 
     lax.fori_loop(0, tiles // 2, own_lookup, 0)
     for copy in forwards:
         copy.wait()
 
-    tabulate(other_highs)
+    other_unscale = tabulate(other_highs)
 
     def other_lookup(u, carry):
         for slot in range(2):
@@ -287,7 +324,7 @@
             pick(t, slot, other_highs)
             decay = jnp.exp(-rate_ref[pl.ds(base, TILE), :])
             for b in range(TILE):
-                mean = choose(t, slot, other_highs, b, state_ref[base + b])[:NS]
+                mean = (state_ref[base + b] + choose(t, slot, other_highs, b) * other_unscale)[:NS]
                 state_ref[base + b, :NS] = mean + (comp_ref[:, base + b, :] - mean) * decay[b : b + 1, :]
                 state_ref[base + b, NS:] = jnp.zeros((ROWS - NS, LANES), f32)
         store_state(u).start()
@@ -310,7 +347,7 @@
     piece = (COLUMNS, ROWS, CELL_DEV)
     outs = (
         jax.ShapeDtypeStruct((blocks, ROWS, LANES), f32),
-        jax.ShapeDtypeStruct((n_gx * COLUMNS, ROWS, LANES), f32),
+        jax.ShapeDtypeStruct((n_gx * COLUMNS, 2 * ROWS, 2 * LANES), bf16),
         jax.ShapeDtypeStruct((8, blocks), jnp.int32),
     )
     return pl.pallas_call(
@@ -323,12 +360,13 @@
             dma((len(args),)),
             dma((blocks // TILE // 2 + 2,)),
             pltpu.VMEM((ROWS, LANES), f32),
-            pltpu.VMEM((blocks // TILE, 2 * ROWS, TILE * LANES), bf16),
-            pltpu.VMEM((blocks // TILE, LOW, TILE * LANES), bf16),
-            pltpu.VMEM((2, HIGHS * 2 * ROWS * 2 // 3, TILE * LANES), bf16),
-            pltpu.VMEM((HIGHS * 2 * ROWS * 2 // 3, LOW), f32),
+            pltpu.VMEM((blocks // TILE, PARTS, TILE * LANES), bf16),
+            pltpu.VMEM((blocks // TILE, LOW, TILE * LANES), f8),
+            pltpu.VMEM((2, HIGHS * PARTS * 2 // 3, TILE * LANES), f8),
+            pltpu.VMEM((HIGHS * PARTS * 2 // 3, LOW), f32),
             pltpu.VMEM((2, HIGHS * ROWS * 2 // 3, TILE * LANES), f32),
-            pltpu.VMEM((2, HIGHS * ROWS * 2 // 3, LOW), bf16),
+            pltpu.VMEM((3, HIGHS * ROWS * 2 // 3, LOW), f8),
+            pltpu.VMEM((3, HIGHS * ROWS * 2 // 3, LOW), f32),
             pltpu.VMEM((2 * COLUMNS, ROWS, CELL_DEV), f32),
             pltpu.VMEM((2, *piece), f32),
             pltpu.VMEM(piece, f32),
@@ -336,7 +374,8 @@
             pltpu.VMEM((ROWS, CELL_DEV), f32),
             pltpu.VMEM((3 * COLUMNS, ROWS, CELL_DEV), f32),
             pltpu.VMEM((COLUMNS, n_gx, PACK, LANES), f32),
-            pltpu.VMEM((3 * LANES, NS // PACK * LANES), f32),
+            pltpu.VMEM((3 * LANES, NS // PACK * 2 * LANES), f32),
+            pltpu.VMEM((n_gx * COLUMNS, ROWS, 2 * LANES), f32),
             dma((2,)), dma((2,)), *[dma((COLUMNS,))] * 8,
             dma((n_gx,)), dma((n_gx,)), dma((COLUMNS,)), dma((COLUMNS,)),
         ],
@@ -347,7 +386,7 @@
 
 
 def react_kernel(plan_ref, *refs):
-    args, (out_ref, state_ref, rates_ref, mats_ref, fetch_sem, pair_ref, turn_ref) = refs[:3], refs[3:]
+    args, (out_ref, state_ref, rates_ref, mats_ref, fetch_sem, pair_ref, half_ref, progress_ref, turn_ref) = refs[:3], refs[3:]
     fetches = [
         pltpu.make_async_copy(src, dst, fetch_sem.at[k])
         for k, (src, dst) in enumerate(zip(args, (state_ref, rates_ref, mats_ref)))
@@ -361,49 +400,55 @@
     for k, piece in enumerate((upper, upper, lower)):
         turn_ref[k * ROWS : k * ROWS + NS, :NR] = piece
     rates = turn_ref[...].T[:STEPS, : 3 * ROWS].astype(bf16)
-    lane = lax.broadcasted_iota(jnp.int32, (ROWS, LANES), 1)
     fetches[0].wait()
     fetches[2].wait()
 
-    def group(g, carry):
-        at = [g * GROUP + b for b in range(GROUP)]
-        block = [plan_ref[1, a] for a in at]
-        need = [plan_ref[2, a] for a in at]
-        for b in range(GROUP):
-            upper, lower = (v.astype(f32) for v in split(mats_ref[plan_ref[0, at[b]]]))
-            turned = pltpu.roll(upper, STEPS, 1)
-            head = jnp.where(lane < STEPS, upper, turned)
-            tail = jnp.where(lane < 2 * STEPS - LANES, turned, 0.0)
-            pair_ref[b, :, :LANES] = jnp.concatenate([head, lower], 0).astype(bf16)
-            pair_ref[b, :, LANES:] = jnp.concatenate([tail, jnp.zeros((ROWS, LANES), f32)], 0).astype(bf16)
-
-        def section(s, states):
-            x = jnp.concatenate(states, 1)
-            upper = x.astype(bf16).astype(f32)
-            progress = jnp.tanh(mm(rates, jnp.concatenate([upper, x - upper, upper], 0).astype(bf16)))
-            upper = progress.astype(bf16).astype(f32)
-            progress = jnp.concatenate([upper, progress - upper], 0).astype(bf16)
-            products = [
-                mm(
-                    pair_ref[b : b + 2].reshape(4 * ROWS, 2 * LANES)[:, : 2 * STEPS],
-                    progress[:, b * LANES : (b + 2) * LANES],
-                )
-                for b in range(0, GROUP, 2)
-            ]
-            after = []
-            for b, y in zip(range(0, GROUP, 2), products):
-                first_change = y[:24, :LANES] + y[24:48, :LANES]
-                second_change = y[48:72, LANES:] + y[72:, LANES:]
-                after.append(jnp.where(s < need[b], states[b] + first_change, states[b]))
-                after.append(jnp.where(s < need[b + 1], states[b + 1] + second_change, states[b + 1]))
-            return tuple(after)
-
-        states = lax.fori_loop(0, need[0], section, tuple(state_ref[b] for b in block))
-        for b in range(GROUP):
-            out_ref[:, block[b], :] = states[b][:NS]
-        return carry
-
-    lax.fori_loop(0, blocks // GROUP, group, 0)
+    def progress(half):
+        x = half_ref[half]
+        upper = x.astype(bf16).astype(f32)
+        value = jnp.tanh(mm(rates, jnp.concatenate([upper, x - upper, upper], 0).astype(bf16)))
+        upper = value.astype(bf16).astype(f32)
+        progress_ref[half] = jnp.concatenate([upper, value - upper], 0).astype(bf16)
+
+    def change(half, s, need):
+        products = [
+            mm(
+                pair_ref[half, b : b + 2].reshape(4 * ROWS, 2 * LANES)[:, : 2 * STEPS],
+                progress_ref[half, :, b * LANES : (b + 2) * LANES],
+            )
+            for b in range(0, GROUP, 2)
+        ]
+        for b, y in zip(range(0, GROUP, 2), products):
+            for c in range(2):
+                lanes = slice((b + c) * LANES, (b + c + 1) * LANES)
+                mine = y[48 * c : 48 * c + 48, c * LANES : (c + 1) * LANES]
+                half_ref[half, :, lanes] += jnp.where(s < need[b + c], mine[:24] + mine[24:], 0.0)
+
+    def two_groups(g, carry):
+        block, need = [], []
+        for half in range(2):
+            at = [(2 * g + half) * GROUP + b for b in range(GROUP)]
+            block.append([plan_ref[1, a] for a in at])
+            need.append([plan_ref[2, a] for a in at])
+            for b in range(GROUP):
+                pair_ref[half, b] = mats_ref[plan_ref[0, at[b]]]
+                half_ref[half, :, b * LANES : (b + 1) * LANES] = state_ref[block[half][b]]
+        progress(0)
+
+        def section(s, carry):
+            change(0, s, need[0])
+            progress(1)
+            progress(0)
+            change(1, s, need[1])
+            return carry
+
+        lax.fori_loop(0, need[0][0], section, 0)
+        for half in range(2):
+            for b in range(GROUP):
+                out_ref[:, block[half][b], :] = half_ref[half, :NS, b * LANES : (b + 1) * LANES]
+        return carry
+
+    lax.fori_loop(0, blocks // (2 * GROUP), two_groups, 0)
 
 
 def react(plan, state, rates, mats):
@@ -416,7 +461,9 @@
         scratch_shapes=[
             *[pltpu.VMEM(a.shape, a.dtype) for a in (state, rates, mats)],
             pltpu.SemaphoreType.DMA((3,)),
-            pltpu.VMEM((GROUP, 2 * ROWS, 2 * LANES), bf16),
+            pltpu.VMEM((2, GROUP, 2 * ROWS, 2 * LANES), bf16),
+            pltpu.VMEM((2, ROWS, GROUP * LANES), f32),
+            pltpu.VMEM((2, 2 * STEPS, GROUP * LANES), bf16),
             pltpu.VMEM((LANES, LANES), f32),
         ],
         compiler_params=pltpu.CompilerParams(vmem_limit_bytes=60 << 20),

time: 66.7 us -> 61.6 us (0.924)
  the two profiles are of different devices: /device:TPU:1 before, /device:TPU:5 now
where the time goes in v5:
time: 61.6 us; the launch traced here: 61.4 us
  Pallas kernels  61.4 us (100%)
    pallas_call x1, Pallas kernels, gather(): pl.pallas_call(functools.partial(gather_kernel, n_gx), out_shape=outs, in...  44.8 us
    pallas_call x1, Pallas kernels, react(): pl.pallas_call(react_kernel, out_shape=jax.ShapeDtypeStruct((NS, blocks,...  16.6 us

profile of v5, /device:TPU:5, one launch (start us, length us, event | category | flops | bytes accessed | tf_op | source)
XLA Modules:
  0.0 61.4 jit_solution(17746352143457029393)
XLA Ops:
  0.0 44.8 %shard_map.91 = (f32[128,24,128]{2,1,0:T(8,128)}, bf16[128,48,256]{2,1,0:T(8,128)(2,1)}, s32[8,128]{1,0:T(8,128)}) custom-call(f32[20,128,128]{2,1,0:T(8,128)} %bitcast.5, f32[128,128]{1,0:T(8,128)} %refs_1_.1, f32[128,128]{1,0:T(8,128)} %refs_2_.1, s32[128,128]{1,0:T(8,128)} %refs_3_.1, s32[1,128]{1,0:T(1,128)} %bitcast.8, s32[1,128]{1,0:T(1,128)} %refs_5_.1, ...), custom_call_target="tpu_custom_call" | custom-call | tf_op jit(solution)/shard_map/pallas_call | solution.py:353
  44.8 16.6 %shard_map.92 = f32[20,128,128]{2,1,0:T(8,128)} custom-call(s32[8,128]{1,0:T(8,128)} %get-tuple-element.8.plan_ref, f32[128,24,128]{2,1,0:T(8,128)} %get-tuple-element.9.refs_0_, f32[20,84]{1,0:T(8,128)} %bitcast.6, bf16[128,48,256]{2,1,0:T(8,128)(2,1)} %get-tuple-element.10.refs_2_), custom_call_target="tpu_custom_call" | custom-call | tf_op jit(solution)/shard_map/pallas_call | solution.py:456

commit v6 on v5

--- a/solution.py
+++ b/solution.py
@@ -22,7 +22,7 @@
 ROWS = 24
 STEPS = 88
 TILE = 8
-GROUP = 16
+GROUP = 32
 STEP_SIZE = 0.25
 PARTS = 64
 TOP = 224.0
@@ -156,20 +156,27 @@
             accumulate(2 * u + slot, slot, other_highs)
         return carry
 
-    lax.fori_loop(0, tiles // 2, other_tiles, 0)
+    lax.fori_loop(0, tiles // 4, other_tiles, 0)
+    pl.semaphore_wait(barrier, len(peers))
+    rows = [
+        send(batch_ref.at[j, i], batch_ref.at[j, i], row_send.at[p], row_recv.at[p], (gx_peer(p), j))
+        for p in range(1, n_gx)
+    ]
+    lax.fori_loop(tiles // 4, tiles // 2, other_tiles, 0)
     for k, even, odd in owners(other_highs):
         part_ref[2 * k] = even
         part_ref[2 * k + 1] = odd
     acc_ref[...] = jnp.zeros_like(acc_ref)
 
-    pl.semaphore_wait(barrier, len(peers))
     halos = [
         send(part_ref.at[pl.ds(0, COLUMNS)], halo_ref.at[1], halo_send.at[0], halo_recv.at[0], (left, j)),
         send(part_ref.at[pl.ds(COLUMNS, COLUMNS)], halo_ref.at[0], halo_send.at[1], halo_recv.at[1], (right, j)),
     ]
-    rows = [
-        send(batch_ref.at[j, i], batch_ref.at[j, i], row_send.at[p], row_recv.at[p], (gx_peer(p), j))
-        for p in range(1, n_gx)
+    for copy in rows:
+        copy.wait()
+    batches = [
+        send(batch_ref.at[j], batch_ref.at[j], batch_send.at[p], batch_recv.at[p], (i, column(p)))
+        for p in range(1, COLUMNS)
     ]
 
     def own_tiles(u, carry):
@@ -178,78 +185,7 @@
             accumulate(2 * u + slot, slot, own_highs)
         return carry
 
-    lax.fori_loop(0, tiles // 4, own_tiles, 0)
-    for copy in rows:
-        copy.wait()
-    batches = [
-        send(batch_ref.at[j], batch_ref.at[j], batch_send.at[p], batch_recv.at[p], (i, column(p)))
-        for p in range(1, COLUMNS)
-    ]
-    lax.fori_loop(tiles // 4, tiles // 2, own_tiles, 0)
-    for copy in halos:
-        copy.wait()
-    for k, even, odd in owners(own_highs):
-        own_ref[2 * k] = even + halo_ref[0, 2 * k] + halo_ref[1, 2 * k]
-        own_ref[2 * k + 1] = odd + halo_ref[0, 2 * k + 1] + halo_ref[1, 2 * k + 1]
-
-    partials = [
-        send(own_ref.at[column(p)], sums_ref.at[p], sum_send.at[p], sum_recv.at[p], (i, column(p)))
-        for p in range(1, COLUMNS)
-    ]
-
-    wide_ref[...] = jnp.zeros_like(wide_ref)
-    upper, lower = (v.astype(f32) for v in split(STEP_SIZE * stoich_ref[...]))
-    for c in range(NS // PACK):
-        for k, piece in enumerate((upper, lower, upper)):
-            for start in (0, STEPS):
-                lanes = slice(2 * c * LANES + start, 2 * c * LANES + start + NR)
-                wide_ref[k * LANES + c * ROWS : k * LANES + c * ROWS + NS, lanes] = piece
-    wide = wide_ref[...].astype(bf16)
-    for copy in batches:
-        copy.wait()
-    batch_total = n_gx * COLUMNS
-    for t in range(PACK):
-        upper, lower = split(batch_ref[:, :, t, :].reshape(batch_total, LANES))
-        product = mm(jnp.concatenate([upper, upper, lower], 1), wide)
-        for c in range(NS // PACK):
-            for side in range(2):
-                at = (2 * c + side) * LANES
-                product_ref[:, PACK * c + t, side * LANES : (side + 1) * LANES] = product[:, at : at + LANES]
-    for r in range(NS, ROWS):
-        product_ref[:, r, :] = jnp.zeros((batch_total, 2 * LANES), f32)
-    once = lax.broadcasted_iota(jnp.int32, (ROWS, 2 * LANES), 1) < STEPS
-
-    def pair(u, carry):
-        for k in range(8):
-            value = product_ref[8 * u + k]
-            upper = value.astype(bf16).astype(f32)
-            mats_ref[8 * u + k] = jnp.concatenate([upper, jnp.where(once, value - upper, 0.0)], 0).astype(bf16)
-        return carry
-
-    lax.fori_loop(0, batch_total // 8, pair, 0)
-    stores = [pltpu.make_async_copy(mats_ref, outs[1], store_sem.at[tiles // 2])]
-    stores[0].start()
-
-    total = own_ref[j]
-    for p, copy in enumerate(partials, 1):
-        copy.wait()
-        total = total + sums_ref[p]
-    means = total[:NS] / total[NS : NS + 1]
-    mine_ref[...] = jnp.concatenate([means, jnp.zeros((ROWS - NS, CELL_DEV), f32)], 0)
-
-    slab_means = [
-        send(mine_ref, near_ref.at[COLUMNS + j], mean_send.at[p], mean_recv.at[p], (i, column(p)))
-        for p in range(1, COLUMNS)
-    ]
-    near_ref[COLUMNS + j] = mine_ref[...]
-
-    def forward(p, src, at):
-        return [
-            send(src, near_ref.at[2 * COLUMNS + at], left_send.at[p], left_recv.at[p], (left, j)),
-            send(src, near_ref.at[at], right_send.at[p], right_recv.at[p], (right, j)),
-        ]
-
-    forwards = forward(0, mine_ref, j)
+    lax.fori_loop(0, tiles // 2, own_tiles, 0)
 
     row = lax.broadcasted_iota(jnp.int32, (blocks, blocks), 0)
     lane = lax.broadcasted_iota(jnp.int32, (blocks, blocks), 1)
@@ -266,7 +202,72 @@
     here = rank == lane_f
     lines = [jnp.sum(jnp.where(here, v, 0.0), axis=0, keepdims=True) for v in (place, block_of, count_of)]
     plan_ref[...] = jnp.concatenate(lines + [jnp.zeros((5, blocks), f32)], 0).astype(jnp.int32)
-    stores.append(pltpu.make_async_copy(plan_ref, outs[2], store_sem.at[tiles // 2 + 1]))
+    stores = [pltpu.make_async_copy(plan_ref, outs[2], store_sem.at[tiles // 2 + 1])]
+    stores[0].start()
+
+    for copy in halos:
+        copy.wait()
+    for k, even, odd in owners(own_highs):
+        own_ref[2 * k] = even + halo_ref[0, 2 * k] + halo_ref[1, 2 * k]
+        own_ref[2 * k + 1] = odd + halo_ref[0, 2 * k + 1] + halo_ref[1, 2 * k + 1]
+
+    partials = [
+        send(own_ref.at[column(p)], sums_ref.at[p], sum_send.at[p], sum_recv.at[p], (i, column(p)))
+        for p in range(1, COLUMNS)
+    ]
+
+    wide_ref[...] = jnp.zeros_like(wide_ref)
+    upper, lower = (v.astype(f32) for v in split(STEP_SIZE * stoich_ref[...]))
+    for c in range(NS // PACK):
+        for k, piece in enumerate((upper, lower, upper)):
+            for start in (0, STEPS):
+                lanes = slice(2 * c * LANES + start, 2 * c * LANES + start + NR)
+                wide_ref[k * LANES + c * ROWS : k * LANES + c * ROWS + NS, lanes] = piece
+    wide = wide_ref[...].astype(bf16)
+    for copy in batches:
+        copy.wait()
+    batch_total = n_gx * COLUMNS
+    for t in range(PACK):
+        upper, lower = split(batch_ref[:, :, t, :].reshape(batch_total, LANES))
+        product = mm(jnp.concatenate([upper, upper, lower], 1), wide)
+        for c in range(NS // PACK):
+            for side in range(2):
+                at = (2 * c + side) * LANES
+                product_ref[:, PACK * c + t, side * LANES : (side + 1) * LANES] = product[:, at : at + LANES]
+    for r in range(NS, ROWS):
+        product_ref[:, r, :] = jnp.zeros((batch_total, 2 * LANES), f32)
+    total = own_ref[j]
+    for p, copy in enumerate(partials, 1):
+        copy.wait()
+        total = total + sums_ref[p]
+    means = total[:NS] / total[NS : NS + 1]
+    mine_ref[...] = jnp.concatenate([means, jnp.zeros((ROWS - NS, CELL_DEV), f32)], 0)
+
+    slab_means = [
+        send(mine_ref, near_ref.at[COLUMNS + j], mean_send.at[p], mean_recv.at[p], (i, column(p)))
+        for p in range(1, COLUMNS)
+    ]
+    near_ref[COLUMNS + j] = mine_ref[...]
+
+    def forward(p, src, at):
+        return [
+            send(src, near_ref.at[2 * COLUMNS + at], left_send.at[p], left_recv.at[p], (left, j)),
+            send(src, near_ref.at[at], right_send.at[p], right_recv.at[p], (right, j)),
+        ]
+
+    forwards = forward(0, mine_ref, j)
+
+    once = lax.broadcasted_iota(jnp.int32, (ROWS, 2 * LANES), 1) < STEPS
+
+    def pair(u, carry):
+        for k in range(8):
+            value = product_ref[8 * u + k]
+            upper = value.astype(bf16).astype(f32)
+            mats_ref[8 * u + k] = jnp.concatenate([upper, jnp.where(once, value - upper, 0.0)], 0).astype(bf16)
+        return carry
+
+    lax.fori_loop(0, batch_total // 8, pair, 0)
+    stores.append(pltpu.make_async_copy(mats_ref, outs[1], store_sem.at[tiles // 2]))
     stores[1].start()
 
     for p, copy in enumerate(slab_means, 1):
@@ -386,7 +387,7 @@
 
 
 def react_kernel(plan_ref, *refs):
-    args, (out_ref, state_ref, rates_ref, mats_ref, fetch_sem, pair_ref, half_ref, progress_ref, turn_ref) = refs[:3], refs[3:]
+    args, (out_ref, state_ref, rates_ref, mats_ref, fetch_sem, turn_ref) = refs[:3], refs[3:]
     fetches = [
         pltpu.make_async_copy(src, dst, fetch_sem.at[k])
         for k, (src, dst) in enumerate(zip(args, (state_ref, rates_ref, mats_ref)))
@@ -394,8 +395,8 @@
     for copy in fetches:
         copy.start()
     blocks = state_ref.shape[0]
+    turn_ref[...] = jnp.zeros_like(turn_ref)
     fetches[1].wait()
-    turn_ref[...] = jnp.zeros_like(turn_ref)
     upper, lower = (v.astype(f32) for v in split(rates_ref[...]))
     for k, piece in enumerate((upper, upper, lower)):
         turn_ref[k * ROWS : k * ROWS + NS, :NR] = piece
@@ -403,52 +404,36 @@
     fetches[0].wait()
     fetches[2].wait()
 
-    def progress(half):
-        x = half_ref[half]
-        upper = x.astype(bf16).astype(f32)
-        value = jnp.tanh(mm(rates, jnp.concatenate([upper, x - upper, upper], 0).astype(bf16)))
-        upper = value.astype(bf16).astype(f32)
-        progress_ref[half] = jnp.concatenate([upper, value - upper], 0).astype(bf16)
-
-    def change(half, s, need):
-        products = [
-            mm(
-                pair_ref[half, b : b + 2].reshape(4 * ROWS, 2 * LANES)[:, : 2 * STEPS],
-                progress_ref[half, :, b * LANES : (b + 2) * LANES],
-            )
-            for b in range(0, GROUP, 2)
-        ]
-        for b, y in zip(range(0, GROUP, 2), products):
-            for c in range(2):
-                lanes = slice((b + c) * LANES, (b + c + 1) * LANES)
-                mine = y[48 * c : 48 * c + 48, c * LANES : (c + 1) * LANES]
-                half_ref[half, :, lanes] += jnp.where(s < need[b + c], mine[:24] + mine[24:], 0.0)
-
-    def two_groups(g, carry):
-        block, need = [], []
-        for half in range(2):
-            at = [(2 * g + half) * GROUP + b for b in range(GROUP)]
-            block.append([plan_ref[1, a] for a in at])
-            need.append([plan_ref[2, a] for a in at])
-            for b in range(GROUP):
-                pair_ref[half, b] = mats_ref[plan_ref[0, at[b]]]
-                half_ref[half, :, b * LANES : (b + 1) * LANES] = state_ref[block[half][b]]
-        progress(0)
-
-        def section(s, carry):
-            change(0, s, need[0])
-            progress(1)
-            progress(0)
-            change(1, s, need[1])
-            return carry
-
-        lax.fori_loop(0, need[0][0], section, 0)
-        for half in range(2):
-            for b in range(GROUP):
-                out_ref[:, block[half][b], :] = half_ref[half, :NS, b * LANES : (b + 1) * LANES]
-        return carry
-
-    lax.fori_loop(0, blocks // (2 * GROUP), two_groups, 0)
+    def group(g, carry):
+        at = [g * GROUP + b for b in range(GROUP)]
+        batch, block, need = ([plan_ref[line, a] for a in at] for line in range(3))
+
+        def section(s, states):
+            x = jnp.concatenate(states, 1)
+            upper = x.astype(bf16).astype(f32)
+            progress = jnp.tanh(mm(rates, jnp.concatenate([upper, x - upper, upper], 0).astype(bf16)))
+            upper = progress.astype(bf16).astype(f32)
+            progress = jnp.concatenate([upper, progress - upper], 0).astype(bf16)
+            products = [
+                mm(
+                    jnp.concatenate([mats_ref[batch[b]], mats_ref[batch[b + 1]]], 0)[:, : 2 * STEPS],
+                    progress[:, b * LANES : (b + 2) * LANES],
+                )
+                for b in range(0, GROUP, 2)
+            ]
+            after = []
+            for b, y in zip(range(0, GROUP, 2), products):
+                for c in range(2):
+                    mine = y[48 * c : 48 * c + 48, c * LANES : (c + 1) * LANES]
+                    after.append(states[b + c] + jnp.where(s < need[b + c], mine[:24] + mine[24:], 0.0))
+            return tuple(after)
+
+        states = lax.fori_loop(0, need[0], section, tuple(state_ref[b] for b in block))
+        for b in range(GROUP):
+            out_ref[:, block[b], :] = states[b][:NS]
+        return carry
+
+    lax.fori_loop(0, blocks // GROUP, group, 0)
 
 
 def react(plan, state, rates, mats):
@@ -461,9 +446,6 @@
         scratch_shapes=[
             *[pltpu.VMEM(a.shape, a.dtype) for a in (state, rates, mats)],
             pltpu.SemaphoreType.DMA((3,)),
-            pltpu.VMEM((2, GROUP, 2 * ROWS, 2 * LANES), bf16),
-            pltpu.VMEM((2, ROWS, GROUP * LANES), f32),
-            pltpu.VMEM((2, 2 * STEPS, GROUP * LANES), bf16),
             pltpu.VMEM((LANES, LANES), f32),
         ],
         compiler_params=pltpu.CompilerParams(vmem_limit_bytes=60 << 20),

time: 61.6 us -> 57.9 us (0.940)
  the two profiles are of different devices: /device:TPU:5 before, /device:TPU:1 now
where the time goes in v6:
time: 57.9 us; the launch traced here: 57.8 us
  Pallas kernels  57.8 us (100%)
    pallas_call x1, Pallas kernels, gather(): pl.pallas_call(functools.partial(gather_kernel, n_gx), out_shape=outs, in...  41.5 us
    pallas_call x1, Pallas kernels, react(): pl.pallas_call(react_kernel, out_shape=jax.ShapeDtypeStruct((NS, blocks,...  16.3 us

profile of v6, /device:TPU:1, one launch (start us, length us, event | category | flops | bytes accessed | tf_op | source)
XLA Modules:
  0.0 57.8 jit_solution(4972588827280191140)
XLA Ops:
  0.0 41.5 %shard_map.91 = (f32[128,24,128]{2,1,0:T(8,128)}, bf16[128,48,256]{2,1,0:T(8,128)(2,1)}, s32[8,128]{1,0:T(8,128)}) custom-call(f32[20,128,128]{2,1,0:T(8,128)} %bitcast.5, f32[128,128]{1,0:T(8,128)} %refs_1_.1, f32[128,128]{1,0:T(8,128)} %refs_2_.1, s32[128,128]{1,0:T(8,128)} %refs_3_.1, s32[1,128]{1,0:T(1,128)} %bitcast.8, s32[1,128]{1,0:T(1,128)} %refs_5_.1, ...), custom_call_target="tpu_custom_call" | custom-call | tf_op jit(solution)/shard_map/pallas_call | solution.py:354
  41.5 16.3 %shard_map.92 = f32[20,128,128]{2,1,0:T(8,128)} custom-call(s32[8,128]{1,0:T(8,128)} %get-tuple-element.8.plan_ref, f32[128,24,128]{2,1,0:T(8,128)} %get-tuple-element.9.refs_0_, f32[20,84]{1,0:T(8,128)} %bitcast.6, bf16[128,48,256]{2,1,0:T(8,128)(2,1)} %get-tuple-element.10.refs_2_), custom_call_target="tpu_custom_call" | custom-call | tf_op jit(solution)/shard_map/pallas_call | solution.py:441

commit v7 on v6

--- a/solution.py
+++ b/solution.py
@@ -21,7 +21,7 @@
 HIGHS = 3 * SLAB // LOW
 ROWS = 24
 STEPS = 88
-TILE = 8
+TILE = 16
 GROUP = 32
 STEP_SIZE = 0.25
 PARTS = 64

time: 57.9 us -> 56.1 us (0.969)
  the two profiles are of different devices: /device:TPU:1 before, /device:TPU:17 now
where the time goes in v7:
time: 56.1 us; the launch traced here: 56 us
  Pallas kernels  55.9 us (100%)
    pallas_call x1, Pallas kernels, gather(): pl.pallas_call(functools.partial(gather_kernel, n_gx), out_shape=outs, in...  39.7 us
    pallas_call x1, Pallas kernels, react(): pl.pallas_call(react_kernel, out_shape=jax.ShapeDtypeStruct((NS, blocks,...  16.3 us

profile of v7, /device:TPU:17, one launch (start us, length us, event | category | flops | bytes accessed | tf_op | source)
XLA Modules:
  0.0 56.0 jit_solution(4002867765426844013)
XLA Ops:
  0.0 39.7 %shard_map.91 = (f32[128,24,128]{2,1,0:T(8,128)}, bf16[128,48,256]{2,1,0:T(8,128)(2,1)}, s32[8,128]{1,0:T(8,128)}) custom-call(f32[20,128,128]{2,1,0:T(8,128)} %bitcast.5, f32[128,128]{1,0:T(8,128)} %refs_1_.1, f32[128,128]{1,0:T(8,128)} %refs_2_.1, s32[128,128]{1,0:T(8,128)} %refs_3_.1, s32[1,128]{1,0:T(1,128)} %bitcast.8, s32[1,128]{1,0:T(1,128)} %refs_5_.1, ...), custom_call_target="tpu_custom_call" | custom-call | tf_op jit(solution)/shard_map/pallas_call | solution.py:354
  39.7 16.3 %shard_map.92 = f32[20,128,128]{2,1,0:T(8,128)} custom-call(s32[8,128]{1,0:T(8,128)} %get-tuple-element.8.plan_ref, f32[128,24,128]{2,1,0:T(8,128)} %get-tuple-element.9.refs_0_, f32[20,84]{1,0:T(8,128)} %bitcast.6, bf16[128,48,256]{2,1,0:T(8,128)(2,1)} %get-tuple-element.10.refs_2_), custom_call_target="tpu_custom_call" | custom-call | tf_op jit(solution)/shard_map/pallas_call | solution.py:441

commit v8 on v7

--- a/solution.py
+++ b/solution.py
@@ -55,8 +55,8 @@
         state_ref, mats_ref, plan_ref, fetch_sem, store_sem, square_ref,
         value_ref, low_ref, spread_ref, acc_ref, pick_ref, table_ref, wide_table_ref, part_ref, halo_ref, own_ref, sums_ref,
         mine_ref, near_ref, batch_ref, wide_ref, product_ref,
-        halo_send, halo_recv, sum_send, sum_recv, mean_send, mean_recv, left_send, left_recv,
-        right_send, right_recv, row_send, row_recv, batch_send, batch_recv,
+        halo_send, halo_recv, sum_send, sum_recv, mean_send, mean_recv, slab_send, slab_recv,
+        row_send, row_recv, batch_send, batch_recv,
     ) = refs[11:]
     fetches = [
         pltpu.make_async_copy(src, dst, fetch_sem.at[k])
@@ -249,14 +249,6 @@
     ]
     near_ref[COLUMNS + j] = mine_ref[...]
 
-    def forward(p, src, at):
-        return [
-            send(src, near_ref.at[2 * COLUMNS + at], left_send.at[p], left_recv.at[p], (left, j)),
-            send(src, near_ref.at[at], right_send.at[p], right_recv.at[p], (right, j)),
-        ]
-
-    forwards = forward(0, mine_ref, j)
-
     once = lax.broadcasted_iota(jnp.int32, (ROWS, 2 * LANES), 1) < STEPS
 
     def pair(u, carry):
@@ -270,10 +262,13 @@
     stores.append(pltpu.make_async_copy(mats_ref, outs[1], store_sem.at[tiles // 2]))
     stores[1].start()
 
-    for p, copy in enumerate(slab_means, 1):
-        copy.wait()
-        source = lax.rem(j - p + COLUMNS, COLUMNS)
-        forwards += forward(p, near_ref.at[COLUMNS + source], source)
+    for copy in slab_means:
+        copy.wait()
+    own = near_ref.at[pl.ds(COLUMNS, COLUMNS)]
+    forwards = [
+        send(own, near_ref.at[pl.ds(2 * COLUMNS, COLUMNS)], slab_send.at[0], slab_recv.at[0], (left, j)),
+        send(own, near_ref.at[pl.ds(0, COLUMNS)], slab_send.at[1], slab_recv.at[1], (right, j)),
+    ]
 
     def tabulate(highs):
         bound = jnp.zeros((ROWS, CELL_DEV), f32)
@@ -377,7 +372,7 @@
             pltpu.VMEM((COLUMNS, n_gx, PACK, LANES), f32),
             pltpu.VMEM((3 * LANES, NS // PACK * 2 * LANES), f32),
             pltpu.VMEM((n_gx * COLUMNS, ROWS, 2 * LANES), f32),
-            dma((2,)), dma((2,)), *[dma((COLUMNS,))] * 8,
+            dma((2,)), dma((2,)), *[dma((COLUMNS,))] * 4, dma((2,)), dma((2,)),
             dma((n_gx,)), dma((n_gx,)), dma((COLUMNS,)), dma((COLUMNS,)),
         ],
         compiler_params=pltpu.CompilerParams(

time: 56.1 us -> 56.6 us (level)
  the two profiles are of different devices: /device:TPU:17 before, /device:TPU:41 now
where the time goes in v8:
time: 56.6 us; the launch traced here: 55.5 us
  Pallas kernels  55.5 us (98%)
    pallas_call x1, Pallas kernels, gather(): pl.pallas_call(functools.partial(gather_kernel, n_gx), out_shape=outs, in...  38.6 us
    pallas_call x1, Pallas kernels, react(): pl.pallas_call(react_kernel, out_shape=jax.ShapeDtypeStruct((NS, blocks,...  16.9 us

profile of v8, /device:TPU:41, one launch (start us, length us, event | category | flops | bytes accessed | tf_op | source)
XLA Modules:
  0.0 55.5 jit_solution(2545888025879253568)
XLA Ops:
  0.0 38.6 %shard_map.91 = (f32[128,24,128]{2,1,0:T(8,128)}, bf16[128,48,256]{2,1,0:T(8,128)(2,1)}, s32[8,128]{1,0:T(8,128)}) custom-call(f32[20,128,128]{2,1,0:T(8,128)} %bitcast.5, f32[128,128]{1,0:T(8,128)} %refs_1_.1, f32[128,128]{1,0:T(8,128)} %refs_2_.1, s32[128,128]{1,0:T(8,128)} %refs_3_.1, s32[1,128]{1,0:T(1,128)} %bitcast.8, s32[1,128]{1,0:T(1,128)} %refs_5_.1, ...), custom_call_target="tpu_custom_call" | custom-call | tf_op jit(solution)/shard_map/pallas_call | solution.py:349
  38.6 16.9 %shard_map.92 = f32[20,128,128]{2,1,0:T(8,128)} custom-call(s32[8,128]{1,0:T(8,128)} %get-tuple-element.8.plan_ref, f32[128,24,128]{2,1,0:T(8,128)} %get-tuple-element.9.refs_0_, f32[20,84]{1,0:T(8,128)} %bitcast.6, bf16[128,48,256]{2,1,0:T(8,128)(2,1)} %get-tuple-element.10.refs_2_), custom_call_target="tpu_custom_call" | custom-call | tf_op jit(solution)/shard_map/pallas_call | solution.py:436
